TPU v7x, 128 devices: a whole 4x4x4 slice. The times are simulated.
128 devices in a mesh: rows: 32 (over z, y, core), cols: 4 (over x).
Axes of the slice: x: 4, y: 4, z: 4, core: 2. Of those that a mesh axis runs over, the one named last changes fastest.
Arguments:
- coupling: float32 [1024, 4, 2, 128, 128], P('rows', 'cols'), may hold values from 1.9 to 2120
- coupling_index: int32 [1024, 4, 2], P('rows', 'cols'), may hold values from 0 to 31, as said below
- near_cost: float32 [1024, 3, 128, 128], P('rows'), may hold values from 0 to 2
- near_index: int32 [1024, 3], P('rows'), may hold values from 0 to 1023, as said below
- source_weights: int32 [131072], P('rows'), may hold values from 1 to 98
- target_cost: float32 [4, 32, 3, 128, 128], P('cols', 'rows'), may hold values from 0 to 2
- target_index: int32 [4, 32, 3], P('cols'), may hold values from 0 to 31, as said below
- target_weights: int32 [4, 4096], P('cols', 'rows'), may hold values from 1 to 98
Outputs:
- cost_blocks: float32 [1024, 4, 2, 128, 128], P('rows', 'cols')
- source_potential: float32 [131072], P('rows')
- target_potential: float32 [4, 4096], P('cols', 'rows')
Inputs may be any that keep to these rules, and one draw needn't show every extreme that they name: `coupling_index`: the 2 entries of one block row and group differ; every target block of every group is named by some block row. near_index[i, 0] = i; the 3 entries of a row differ and lie in the same aligned group of 4 block rows as i. target_index[c, j, 0] = j; the 3 entries of a row differ.
All inputs are finite; a program needn't handle non-finite values.
Results may differ from a plain program's by a relative error of at most 0.0003.
Values sent between devices are 32-bit elements; how exact they have to be, the bound alone decides.
A program may use at most 256 MiB of HBM per device.

v0:
```python
import jax
import jax.numpy as jnp
from jax import lax
from jax.sharding import PartitionSpec as P

ITERS = 3


entropy = 0.01
very_low = -1e30
full_precision = lax.Precision.HIGHEST


def per_device(
    coupling,
    coupling_index,
    near_cost,
    near_index,
    source_weights,
    target_cost,
    target_index,
    target_weights,
):
    rows_here = coupling.shape[0]
    slot_count = coupling.shape[2]
    width = coupling.shape[3]
    near_count = near_cost.shape[1]
    group_blocks = target_index.shape[1]
    link_count = target_index.shape[2]
    target_here = target_cost.shape[1]
    row_devices = lax.axis_size("rows")
    col_devices = lax.axis_size("cols")
    first_row = lax.axis_index("rows") * rows_here
    source_count = rows_here * row_devices * width
    target_count = group_blocks * width * col_devices
    source_float = source_weights.astype(jnp.float32)
    source_total = lax.psum(jnp.sum(source_float), "rows")
    source_mass = (source_count * source_float / source_total).reshape(rows_here, width)
    group_cost, group_weights = (
        lax.all_gather(target_cost, "rows", axis=1, tiled=True),
        lax.all_gather(target_weights.astype(jnp.float32), "rows", axis=1, tiled=True),
    )
    target_total = lax.psum(jnp.sum(group_weights), "cols")
    target_mass = (target_count * group_weights[0] / target_total).reshape(group_blocks, width)
    group_cost = group_cost[0]
    links = target_index[0]
    scale_near = 1.0 / (near_count * width)
    scale_far = 1.0 / (slot_count * col_devices * width)
    local_near = near_index - first_row
    row_term = (
        jnp.einsum(
            "ikxy,iky->ix", near_cost * near_cost, source_mass[local_near], precision=full_precision
        )
        * scale_near
    )
    spread_terms = jnp.einsum(
        "jw,jmwz->jmz", target_mass, group_cost * group_cost, precision=full_precision
    )
    one_hot = (links[..., None] == jnp.arange(group_blocks)[None, None, :]).astype(jnp.float32)
    column_term = jnp.einsum("jmz,jmt->tz", spread_terms, one_hot, precision=full_precision) / (
        link_count * width
    )
    slots_here = coupling_index[:, 0, :]
    far_plan = coupling[local_near][:, :, 0]
    partial_blocks = jnp.einsum("ikxy,ikqyz->ikqxz", near_cost, far_plan, precision=full_precision)
    far_slots = slots_here[local_near]
    far_blocks = group_cost[far_slots]
    match = (links[far_slots][..., None] == slots_here[:, None, None, None, :]).astype(jnp.float32)
    through = jnp.einsum(
        "ikqxy,ikqmyz->ikqmxz", partial_blocks, far_blocks, precision=full_precision
    )
    product = jnp.einsum("ikqmxz,ikqml->ilxz", through, match, precision=full_precision)
    cost_blocks = (
        row_term[:, None, :, None]
        + column_term[slots_here][:, :, None, :]
        - 2.0 * scale_near * scale_far * product
    )
    log_source = jnp.log(source_mass)
    log_target = jnp.log(target_mass)
    selected = slots_here[..., None] == jnp.arange(group_blocks)[None, None, :]
    selected_float = selected.astype(jnp.float32)
    target_potential = jnp.zeros((group_blocks, width), jnp.float32)
    source_potential = jnp.zeros((rows_here, width), jnp.float32)
    for step in range(ITERS):
        scores = (target_potential[slots_here][:, :, None, :] - cost_blocks) / entropy
        row_peak = jnp.max(scores, axis=(1, 3))
        row_peak = lax.pmax(row_peak, "cols")
        row_part = jnp.sum(jnp.exp(scores - row_peak[:, None, :, None]), axis=(1, 3))
        row_total = lax.psum(row_part, "cols")
        source_potential = entropy * (log_source - (row_peak + jnp.log(row_total)))
        back_scores = (source_potential[:, None, :, None] - cost_blocks) / entropy
        slot_peak = jnp.max(back_scores, axis=2)
        column_peak = jnp.max(
            jnp.where(selected[..., None], slot_peak[:, :, None, :], very_low), axis=(0, 1)
        )
        column_peak = lax.pmax(column_peak, "rows")
        slot_total = jnp.sum(jnp.exp(back_scores - column_peak[slots_here][:, :, None, :]), axis=2)
        column_part = jnp.einsum(
            "iqt,iqz->tz", selected_float, slot_total, precision=full_precision
        )
        column_total = lax.psum(column_part, "rows")
        target_potential = entropy * (log_target - (column_peak + jnp.log(column_total)))
    own_target = lax.dynamic_slice_in_dim(
        target_potential, lax.axis_index("rows") * target_here, target_here, 0
    )
    return (cost_blocks[:, None], source_potential.reshape(rows_here * width), own_target)


def solution(mesh):
    placed = (
        P("rows", "cols", None, None, None),
        P("rows", "cols", None),
        P("rows", None, None, None),
        P("rows", None),
        P("rows"),
        P("cols", "rows", None, None, None),
        P("cols", None, None),
        P("cols", "rows"),
    )
    return jax.shard_map(
        per_device,
        mesh=mesh,
        in_specs=placed,
        out_specs=(P("rows", "cols", None, None, None), P("rows"), P("cols", "rows")),
        check_vma=False,
    )
```

profile of v0, /device:TPU:1, one launch (start us, length us, event | category | flops | bytes accessed | tf_op | source)
XLA Modules:
  0.0 1509.0 jit_solution(17361804279378400418)
XLA Ops:
  7.2 0.7 all-gather.2.cloned.1.call-update
  7.9 0.7 convert_element_type.10
  8.6 24.2 %all_gather.6 = f32[1,4096]{1,0:T(1,128)S(1)} all-gather(f32[1,128]{1,0:T(1,128)S(1)} %convert_element_type.10), channel_id=1, replica_groups=mesh['rows'=32,'cols'=4] {'rows'}, dimensions={1}, use_global_device_ids=true | all-gather | bytes 16896 | tf_op jit(solution)/shard_map/all_gather | solution.py:41
  32.8 1.3 convert_reduce_fusion
  34.7 63.1 %psum.56 = f32[]{:T(128)} all-reduce(f32[]{:T(128)} %convert_reduce_fusion), channel_id=1, replica_groups=mesh['rows'=32,'cols'=4] {'rows'}, use_global_device_ids=true, to_apply=%region_1.0 | all-reduce | flops 1 | bytes 8 | tf_op jit(solution)/shard_map/psum | solution.py:37
  97.9 9.4 psum.57
  107.3 0.7 copy.81
  107.9 0.8 copy.46
  108.7 0.7 iota_compare_fusion.2
  109.5 0.7 compare_select_fusion.1
  110.4 0.7 compare_select_fusion.2
  111.4 1.4 divide_bitcast_fusion
  114.6 10.9 gather_fusion.5
  126.2 0.7 gather_fusion.3
  126.9 8.9 fusion.5
  136.0 0.7 multiply_divide_fusion
  136.6 27.6 %fusion.1 = f32[32,3,2,128,128]{4,3,2,1,0:T(8,128)} fusion(f32[32,3,2,128,128]{4,3,2,1,0:T(8,128)} %bitcast.100, f32[32,3,128,128]{3,2,1,0:T(8,128)} %param.10), kind=kOutput, calls=%fused_computation.14 | convolution fusion | flops 4831838208 | bytes 31457280 | tf_op jit(solution)/shard_map/ikxy,ikqyz->ikqxz/dot_general | solution.py:65
  164.2 5.8 fusion.3
  170.9 20.0 %gather_fusion.4 = f32[192,3,128,128]{3,2,1,0:T(8,128)} fusion(f32[32,3,128,128]{3,2,1,0:T(8,128)} %bitcast.98, s32[1024]{0:T(1024)S(1)} %pad_clamp_fusion), kind=kCustom, calls=%fused_computation.4 | custom fusion | bytes 75498240 | tf_op jit(solution)/shard_map/gather | solution.py:67
  190.9 69.4 %convolution_bitcast_fusion = f32[32,3,2,3,128,128]{4,5,3,2,1,0:T(8,128)} fusion(f32[32,3,2,3,128,128]{5,4,3,2,1,0:T(8,128)} %bitcast.99, f32[32,3,2,128,128]{4,3,2,1,0:T(8,128)} %fusion.1), kind=kOutput, calls=%fused_computation.12 | convolution fusion | flops 14495514624 | bytes 88080384 | tf_op jit(solution)/shard_map/ikqxy,ikqmyz->ikqmxz/dot_general | solution.py:69
  260.2 50.0 %copy.53 = f32[32,3,2,3,128,128]{5,3,2,1,4,0:T(4,128)} copy(f32[32,3,2,3,128,128]{4,5,3,2,1,0:T(8,128)} %convolution_bitcast_fusion) | data formatting | bytes 75497472 | tf_op jit(solution)/shard_map/ikqxy,ikqmyz->ikqmxz/transpose | solution.py:69
  310.2 99.7 %fusion.8 = (f32[32,128]{1,0:T(8,128)S(1)}, f32[32,2,128,128]{3,1,2,0:T(2,128)}) fusion(f32[32,2,128]{2,1,0:T(2,128)S(1)} %bitcast.112, f32[32,3,2,3,128,128]{5,3,2,1,4,0:T(4,128)} %copy.53, f32[32,2,128]{2,1,0:T(2,128)S(1)} %bitcast.123, f32[32,128]{1,0:T(8,128)S(1)} %broadcast_multiply_fusion, pred[32,3,2,3,2,1]{3,4,2,1,5,0:T(4,128)(4,1)S(1)} %fusion.15.clone.4), kind=kOutput, calls=%fused_computation.34 | convolution fusion | flops 232779776 | bytes 42042496 | tf_op jit(solution)/shard_map/ikqmxz,ikqml->ilxz/dot_general | solution.py:72
  410.0 11.1 pmax.42
  421.0 60.5 %exponential_reduce_fusion.5 = f32[32,128]{1,0:T(8,128)S(1)} fusion(f32[32,2,128,128]{3,1,2,0:T(2,128)} %get-tuple-element.18, f32[32,128]{1,0:T(8,128)S(1)} %pmax.42, f32[32,2,128]{2,1,0:T(2,128)S(1)} %bitcast.113), kind=kLoop, calls=%fused_computation.32 | loop fusion | flops 4190208 | bytes 4259840 | tf_op jit(solution)/shard_map/reduce_sum | solution.py:88
  481.6 11.2 psum.58
  492.8 0.7 subtract_multiply_fusion.10
  493.5 7.4 fusion.9
  501.2 130.0 %pmax.43 = f32[32,128]{1,0:T(8,128)S(1)} all-reduce(f32[32,128]{1,0:T(8,128)S(1)} %select_reduce_fusion.2), channel_id=1, replica_groups=mesh['rows'=32,'cols'=4] {'rows'}, use_global_device_ids=true, to_apply=%region_10.11 | all-reduce | flops 4096 | bytes 32768 | tf_op jit(solution)/shard_map/pmax | solution.py:96
  631.9 7.4 exponential_reduce_fusion.4
  639.5 123.9 %psum.59 = f32[32,128]{1,0:T(8,128)S(1)} all-reduce(f32[32,128]{1,0:T(8,128)S(1)} %convolution_bitcast_fusion.3), channel_id=1, replica_groups=mesh['rows'=32,'cols'=4] {'rows'}, use_global_device_ids=true, to_apply=%region_12.13 | all-reduce | flops 4096 | bytes 32768 | tf_op jit(solution)/shard_map/psum | solution.py:101
  764.1 11.2 fusion.10
  775.2 10.8 pmax.44
  786.0 60.5 %exponential_reduce_fusion.3 = f32[32,128]{1,0:T(8,128)S(1)} fusion(f32[32,2,128,128]{3,1,2,0:T(2,128)} %get-tuple-element.18, f32[32,128]{1,0:T(8,128)S(1)} %pmax.44, f32[32,2,128]{2,1,0:T(2,128)S(1)} %bitcast.104), kind=kLoop, calls=%fused_computation.28 | loop fusion | flops 4190208 | bytes 4259840 | tf_op jit(solution)/shard_map/reduce_sum | solution.py:88
  846.6 11.7 psum.60
  858.3 0.7 subtract_multiply_fusion.8
  858.9 7.4 fusion.11
  866.7 131.3 %pmax.45 = f32[32,128]{1,0:T(8,128)S(1)} all-reduce(f32[32,128]{1,0:T(8,128)S(1)} %select_reduce_fusion.1), channel_id=1, replica_groups=mesh['rows'=32,'cols'=4] {'rows'}, use_global_device_ids=true, to_apply=%region_19.20 | all-reduce | flops 4096 | bytes 32768 | tf_op jit(solution)/shard_map/pmax | solution.py:96
  998.6 7.4 exponential_reduce_fusion.2
  1006.2 123.8 %psum.61 = f32[32,128]{1,0:T(8,128)S(1)} all-reduce(f32[32,128]{1,0:T(8,128)S(1)} %convolution_bitcast_fusion.2), channel_id=1, replica_groups=mesh['rows'=32,'cols'=4] {'rows'}, use_global_device_ids=true, to_apply=%region_21.22 | all-reduce | flops 4096 | bytes 32768 | tf_op jit(solution)/shard_map/psum | solution.py:101
  1130.6 11.2 fusion.12
  1141.8 11.1 pmax.46
  1152.8 60.5 %exponential_reduce_fusion.1 = f32[32,128]{1,0:T(8,128)S(1)} fusion(f32[32,2,128,128]{3,1,2,0:T(2,128)} %get-tuple-element.18, f32[32,128]{1,0:T(8,128)S(1)} %pmax.46, f32[32,2,128]{2,1,0:T(2,128)S(1)} %bitcast.106), kind=kLoop, calls=%fused_computation.24 | loop fusion | flops 4190208 | bytes 4259840 | tf_op jit(solution)/shard_map/reduce_sum | solution.py:88
  1213.4 11.5 psum.62
  1225.5 7.4 fusion.13
  1233.3 131.3 %pmax.47 = f32[32,128]{1,0:T(8,128)S(1)} all-reduce(f32[32,128]{1,0:T(8,128)S(1)} %select_reduce_fusion), channel_id=1, replica_groups=mesh['rows'=32,'cols'=4] {'rows'}, use_global_device_ids=true, to_apply=%region_28.29 | all-reduce | flops 4096 | bytes 32768 | tf_op jit(solution)/shard_map/pmax | solution.py:96
  1365.2 7.4 exponential_reduce_fusion
  1372.8 123.8 %psum.63 = f32[32,128]{1,0:T(8,128)S(1)} all-reduce(f32[32,128]{1,0:T(8,128)S(1)} %convolution_bitcast_fusion.1), channel_id=1, replica_groups=mesh['rows'=32,'cols'=4] {'rows'}, use_global_device_ids=true, to_apply=%region_30.31 | all-reduce | flops 4096 | bytes 32768 | tf_op jit(solution)/shard_map/psum | solution.py:101
  1496.6 4.8 copy.58
  (46 shorter events, 10.6 us)
Async XLA Ops:
  7.2 157.1 %all-gather.2.cloned.1.call-start = ((), (), s32[]{:S(2)}) async-start(), calls=%async_computation | async-start | bytes 6488064 | tf_op jit(solution)/shard_map/all_gather | solution.py:40
  409.9 82.9 %copy-start = (s32[4096]{0:T(1024)S(1)}, s32[4096]{0:T(1024)}, u32[]{:S(2)}) copy-start(s32[4096]{0:T(1024)} %param.12) | copy-start | bytes 49156
  493.5 145.8 %copy-start.2 = (s32[32,1,2]{0,2,1:T(2,128)S(1)}, s32[32,1,2]{0,2,1:T(2,128)}, u32[]{:S(2)}) copy-start(s32[32,1,2]{0,2,1:T(2,128)} %param.9) | copy-start | bytes 772
  1225.5 147.1 %copy-start.1 = (f32[32,128]{1,0:T(8,128)}, f32[32,128]{1,0:T(8,128)S(1)}, u32[]{:S(2)}) copy-start(f32[32,128]{1,0:T(8,128)S(1)} %subtract_multiply_fusion.6) | copy-start | bytes 49156
Sparse Core Ops, SparseCore 0:
  10.2 53.0 all-gather.1
where the time goes:
time: 1520 us; the launch traced here: 1510 us
  blocking collectives  928 us (61%)
  other arithmetic  259 us (17%)
  matrix products  212 us (14%)
  local copies, waits for them, and re-layouts  94.4 us (6%)
    pmax x3, blocking collectives, per_device(): column_peak = lax.pmax(column_peak, 'rows')  393 us
    psum x3, blocking collectives, per_device(): column_total = lax.psum(column_part, 'rows')  371 us
    reduce_sum x3, other arithmetic, per_device(): jnp.sum(jnp.exp(scores - row_peak[:, None, :, None]), axis=(1, 3))  182 us
    dot_general x1, matrix products, per_device(): jnp.einsum('ikqmxz,ikqml->ilxz', through, match, precision=full_precision)  99.7 us
    dot_general x1, matrix products, per_device(): jnp.einsum('ikqxy,ikqmyz->ikqmxz', partial_blocks, far_blocks, precision=...  69.4 us
    psum x1, blocking collectives, per_device(): source_total = lax.psum(jnp.sum(source_float), 'rows')  63.1 us
    transpose x1, local copies, waits for them, and re-layouts, per_device(): jnp.einsum('ikqxy,ikqmyz->ikqmxz', partial_blocks, far_blocks, precision=...  50 us
    psum x3, blocking collectives, per_device(): row_total = lax.psum(row_part, 'cols')  34.3 us
  transfers between devices with their start and end apart: 1, of which 0 were waited for; matrix products, arithmetic and copies ran while one was open for 4% of the time, Pallas kernels for 0%

commit v1 on v0

v1 whole, which is shorter than its diff:
```python
import functools

import jax
import jax.numpy as jnp
from jax import lax
from jax.experimental import pallas as pl
from jax.experimental.pallas import tpu as pltpu
from jax.sharding import PartitionSpec as P

MESH = pl.DeviceIdType.MESH
BLK = 128
ROWS = 32
NEAR = 3
LINKS = 3
SLOTS = 2
GB = 32
ITERS = 3
SHARD = LINKS * BLK
HALF = SHARD // 2
QUARTER = SHARD // 4
COLS = 4
ENTROPY = 0.01
LOW = -1e30
f32 = jnp.float32
bf16 = jnp.bfloat16


def gather_plan():
    pieces = []
    for dz in range(4):
        for dy in range(4):
            if dz == 0 and dy == 0:
                continue
            for half in range(2):
                low = half * HALF
                if half == 0:
                    axis = "z" if dz else "y"
                else:
                    axis = "y" if dy else "z"
                far = dz if axis == "z" else dy
                if far == 1:
                    cuts = [(1, low, HALF)]
                elif far == 3:
                    cuts = [(-1, low, HALF)]
                else:
                    cuts = [(-1, low, QUARTER), (1, low + QUARTER, QUARTER)]
                hops = min(dz, 4 - dz) + min(dy, 4 - dy)
                for side, first, size in cuts:
                    pieces.append((hops, half, dz, dy, first, size, axis, side))
    pieces.sort(key=lambda p: (p[0], p[2] != 0 if p[1] == 0 else p[3] != 0, p[5] != HALF, p[2], p[3], p[1]))
    return pieces


PIECES = gather_plan()


def split(value):
    high = value.astype(bf16)
    return high, (value - high.astype(f32)).astype(bf16)


def dot(a, b):
    return jnp.dot(a, b, preferred_element_type=f32)


def kernel(
    slots,
    near,
    links,
    source_ref,
    weight_ref,
    coupling_hbm,
    near_hbm,
    target_hbm,
    cost_hbm,
    source_out,
    target_out,
    near_cost,
    plan,
    plan_high,
    plan_low,
    partial,
    row_sum,
    gathered,
    far_high,
    far_low,
    cost,
    scaled,
    source_float,
    source_rows,
    weight_float,
    weight_land,
    extra,
    column,
    log_source,
    log_target,
    row_lse,
    row_land,
    source_pot,
    half_out,
    half_land,
    merged,
    merged_land,
    target_pot,
    peaks,
    sums,
    load_sem,
    gather_send,
    gather_recv,
    pair_send,
    pair_recv,
    early_send,
    early_recv,
    extra_send,
    extra_recv,
    row_send,
    row_recv,
    half_send,
    half_recv,
    merge_send,
    merge_recv,
    pot_send,
    pot_recv,
):
    rank = lax.axis_index("rows")
    group = lax.axis_index("cols")
    z = rank // 8
    y = (rank // 2) % 4
    core = rank % 2

    def at(dz, dy, other=0):
        return (((z + dz) % 4) * 4 + (y + dy) % 4) * 2 + (core + other) % 2

    def device(dz, dy, other=0, dx=0):
        return (at(dz, dy, other), (group + dx) % COLS)

    def remote(src, dst, send, recv, where):
        return pltpu.make_async_remote_copy(
            src_ref=src, dst_ref=dst, send_sem=send, recv_sem=recv, device_id=where, device_id_type=MESH
        )

    def shard_rows(dz, dy, first, size, other=0):
        return gathered.at[pl.ds(pl.multiple_of(at(dz, dy, other) * SHARD + first, 8), size)]

    loads = []
    chunk = ROWS // 4
    for part in range(4):
        loads.append(
            pltpu.make_async_copy(
                coupling_hbm.at[pl.ds(part * chunk * SLOTS, chunk * SLOTS)],
                plan.at[pl.ds(part * chunk * SLOTS, chunk * SLOTS)],
                load_sem.at[part],
            )
        )
    for part in range(4):
        loads.append(
            pltpu.make_async_copy(
                near_hbm.at[pl.ds(part * chunk * NEAR, chunk * NEAR)],
                near_cost.at[pl.ds(part * chunk * NEAR, chunk * NEAR)],
                load_sem.at[4 + part],
            )
        )
    own_rows = gathered.at[pl.ds(pl.multiple_of(rank * SHARD, 8), SHARD)]
    own_load = pltpu.make_async_copy(target_hbm, own_rows, load_sem.at[8])
    own_load.start()

    barrier = pltpu.get_barrier_semaphore()
    neighbours = [device(0, 0, 1), device(0, 1), device(0, 3), device(1, 0), device(3, 0)]
    neighbours += [device(0, 0, 0, dx) for dx in (1, 2, 3)]
    for where in neighbours:
        pl.semaphore_signal(barrier, inc=1, device_id=where, device_id_type=MESH)
    weight_float[...] = weight_ref[...].astype(f32)
    source_float[...] = source_ref[...].astype(f32)
    source_rows[...] = source_float[...].reshape(ROWS, 1, BLK)
    pl.semaphore_wait(barrier, len(neighbours))

    started = []

    def start(copy):
        copy.start()
        started.append(copy)

    held = set()
    sent = set()

    def send_ready():
        for number, (hops, half, dz, dy, first, size, axis, side) in enumerate(PIECES):
            if number in sent:
                continue
            from_z, from_y = (((dz - side) % 4), dy) if axis == "z" else (dz, ((dy - side) % 4))
            if from_z == 0 and from_y == 0:
                src = target_hbm.at[pl.ds(first, size)]
            else:
                covered = sum(
                    p[5]
                    for n, p in enumerate(PIECES)
                    if n in held
                    and (p[2], p[3]) == (from_z, from_y)
                    and p[4] < first + size
                    and first < p[4] + p[5]
                )
                if covered < size:
                    continue
                src = shard_rows(from_z, from_y, first, size)
            dst = shard_rows(from_z, from_y, first, size)
            where = device(-side, 0) if axis == "z" else device(0, -side)
            start(remote(src, dst, gather_send.at[number], gather_recv.at[number], where))
            sent.add(number)

    def take(number):
        hops, half, dz, dy, first, size, axis, side = PIECES[number]
        here = shard_rows(dz, dy, first, size)
        remote(here, here, gather_send.at[number], gather_recv.at[number], device(0, 0, 1)).wait_recv()
        held.add(number)
        send_ready()
        start(remote(here, here, pair_send.at[number], pair_recv.at[number], device(0, 0, 1)))

    def take_level(hops):
        for number, piece in enumerate(PIECES):
            if piece[0] == hops:
                take(number)

    send_ready()
    pair_own = len(PIECES)
    start(remote(target_hbm, own_rows, pair_send.at[pair_own], pair_recv.at[pair_own], device(0, 0, 1)))
    for copy in loads:
        copy.start()
    for dx in (1, 2, 3):
        start(
            remote(weight_float, weight_land.at[dx], early_send.at[dx], early_recv.at[dx], device(0, 0, 0, dx))
        )

    def slot_at(row, slot):
        wanted = slots[slot, row]
        return lax.rem(wanted, 2) * 16 + lax.div(wanted, 2)

    def block_at(far, wanted):
        found = jnp.int32(GB * LINKS)
        for link in range(LINKS):
            found = jnp.where(links[link, 0, far] == wanted, far * LINKS + link, found)
        return found

    def split_plan(row, _):
        for q in range(SLOTS):
            high, low = split(plan[row * SLOTS + q])
            plan_high[row, :, q * BLK : (q + 1) * BLK] = high
            plan_low[row, :, q * BLK : (q + 1) * BLK] = low
        return 0

    def first_product(row, _):
        total = jnp.zeros((BLK, BLK), f32)
        for k in range(NEAR):
            other = lax.rem(near[k, row], ROWS)
            block = near_cost[row * NEAR + k]
            high, low = split(block)
            high_plan = plan_high[other]
            low_plan = plan_low[other]
            both = jnp.concatenate([high, low], axis=1)
            result = dot(both, jnp.concatenate([high_plan, high_plan], axis=0)) + dot(high, low_plan)
            result_high, result_low = split(result)
            partial[row, 0:BLK, k * 2 * BLK : (k + 1) * 2 * BLK] = result_high
            partial[row, BLK : 2 * BLK, k * 2 * BLK : (k + 1) * 2 * BLK] = result_low
            total = total + block * block * source_rows[other]
        row_sum[row] = jnp.broadcast_to(jnp.sum(total, axis=1, keepdims=True), (BLK, BLK))
        return 0

    def first_rows(low, high):
        for part in range(4):
            if low <= part * chunk < high:
                loads[4 + part].wait()
        lax.fori_loop(low, high, first_product, 0)

    for part in range(4):
        loads[part].wait()
        lax.fori_loop(part * chunk, (part + 1) * chunk, split_plan, 0)
    first_rows(0, 4)
    take_level(1)

    own_load.wait()
    own_weight = weight_float[...]
    weight_column = jnp.broadcast_to(own_weight, (BLK, BLK)).T
    extra_rows = [own_weight]
    for link in range(LINKS):
        block = gathered[pl.ds(pl.multiple_of(rank * SHARD + link * BLK, 8), BLK), :]
        extra_rows.append(jnp.sum(block * block * weight_column, axis=0, keepdims=True))
    across = own_weight
    for dx in (1, 2, 3):
        remote(
            weight_float, weight_land.at[dx], early_send.at[dx], early_recv.at[dx], device(0, 0, 0, dx)
        ).wait_recv()
        across = across + weight_land[dx]
    extra_rows.append(across)
    extra_rows.append(jnp.sum(source_float[...], axis=0, keepdims=True))
    extra_rows.append(jnp.zeros((2, BLK), f32))
    extra[core, z, y] = jnp.concatenate(extra_rows, axis=0)

    first_rows(4, 12)
    take_level(2)
    own_extra = extra.at[core, z, y]
    for dy in (1, 2, 3):
        start(remote(own_extra, own_extra, extra_send.at[dy], extra_recv.at[dy], device(0, dy)))
    first_rows(12, 24)
    for dy in (1, 2, 3):
        remote(own_extra, own_extra, extra_send.at[dy], extra_recv.at[dy], device(0, dy)).wait_recv()
    own_extra = extra.at[core, z]
    for dz in (1, 2, 3):
        start(remote(own_extra, own_extra, extra_send.at[3 + dz], extra_recv.at[3 + dz], device(dz, 0)))
    take_level(3)
    first_rows(24, 32)
    for dz in (1, 2, 3):
        remote(own_extra, own_extra, extra_send.at[3 + dz], extra_recv.at[3 + dz], device(dz, 0)).wait_recv()
    own_extra = extra.at[core]
    start(remote(own_extra, own_extra, extra_send.at[0], extra_recv.at[0], device(0, 0, 1)))
    take_level(4)

    for number, piece in enumerate(PIECES):
        here = shard_rows(piece[2], piece[3], piece[4], piece[5], 1)
        remote(here, here, pair_send.at[number], pair_recv.at[number], device(0, 0, 1)).wait_recv()
    here = shard_rows(0, 0, 0, SHARD, 1)
    remote(here, here, pair_send.at[pair_own], pair_recv.at[pair_own], device(0, 0, 1)).wait_recv()
    remote(own_extra, own_extra, extra_send.at[0], extra_recv.at[0], device(0, 0, 1)).wait_recv()

    def split_far(step, _):
        rows = pl.multiple_of(step * SHARD, SHARD)
        for link in range(LINKS):
            high, low = split(gathered[pl.ds(rows + link * BLK, BLK), :])
            far_high[step * LINKS + link] = high
            far_low[step * LINKS + link] = low
        return 0

    lax.fori_loop(0, GB, split_far, 0)
    far_high[GB * LINKS] = jnp.zeros((BLK, BLK), bf16)
    far_low[GB * LINKS] = jnp.zeros((BLK, BLK), bf16)

    everything = extra[...].reshape(GB, 8, BLK)
    target_total = jnp.sum(everything[:, 4, :])
    source_total = jnp.sum(everything[:, 5, :])
    target_scale = (COLS * GB * BLK) / target_total
    source_scale = (GB * ROWS * BLK) / source_total
    log_source[...] = jnp.log(source_float[...] * source_scale)
    log_target[...] = jnp.log(everything[:, 0, :] * target_scale)
    column_scale = target_scale / (LINKS * BLK)
    row_scale = source_scale / (NEAR * BLK)
    position = lax.broadcasted_iota(jnp.int32, (GB, BLK), 0)

    def add_column(step, total):
        own = (step % 16) * 2 + step // 16
        for link in range(LINKS):
            lands = links[link, 0, own]
            lands = lax.rem(lands, 2) * 16 + lax.div(lands, 2)
            value = extra[step // 16, (step // 4) % 4, step % 4, 1 + link : 2 + link, :]
            total = total + jnp.where(position == lands, value, 0.0)
        return total

    column_term = lax.fori_loop(0, GB, add_column, jnp.zeros((GB, BLK), f32)) * column_scale
    column[...] = column_term.reshape(GB, 1, BLK)

    factor = 2.0 / (NEAR * BLK) / (COLS * SLOTS * BLK)

    def second_product(row, _):
        high_rows = []
        low_rows = []
        wanted = [slots[slot, row] for slot in range(SLOTS)]
        for k in range(NEAR):
            other = lax.rem(near[k, row], ROWS)
            for q in range(SLOTS):
                far = slots[q, other]
                found = [block_at(far, wanted[slot]) for slot in range(SLOTS)]
                high_rows.append(jnp.concatenate([far_high[n] for n in found], axis=1))
                low_rows.append(jnp.concatenate([far_low[n] for n in found], axis=1))
        result = dot(partial[row], jnp.concatenate(high_rows, axis=0))
        result = result[0:BLK] + result[BLK : 2 * BLK]
        result = result + dot(partial[row, 0:BLK, :], jnp.concatenate(low_rows, axis=0))
        across = row_sum[row] * row_scale
        for slot in range(SLOTS):
            own_column = column[slot_at(row, slot)]
            value = across + own_column - factor * result[:, slot * BLK : (slot + 1) * BLK]
            cost[row * SLOTS + slot] = value
            scaled[row * SLOTS + slot] = value * (1.0 / ENTROPY)
        return 0

    lax.fori_loop(0, ROWS, second_product, 0)
    out_copy = pltpu.make_async_copy(cost, cost_hbm, load_sem.at[9])
    out_copy.start()

    target_pot[0] = jnp.zeros((GB, 1, BLK), f32)
    mine = core * 16
    theirs = 16 - mine

    def row_pass(step):
        def body(part, _):
            tops = []
            totals = []
            for inner in range(8):
                row = part * 8 + inner
                scores = []
                for slot in range(SLOTS):
                    potential = target_pot[step, slot_at(row, slot)]
                    scores.append(potential - scaled[row * SLOTS + slot])
                top = jnp.max(jnp.maximum(scores[0], scores[1]), axis=1, keepdims=True)
                total = jnp.sum(jnp.exp(scores[0] - top) + jnp.exp(scores[1] - top), axis=1, keepdims=True)
                tops.append(top)
                totals.append(total)
            tops = jnp.concatenate(tops, axis=1).T
            totals = jnp.concatenate(totals, axis=1).T
            row_lse[step, pl.ds(pl.multiple_of(part * 8, 8), 8), :] = tops + jnp.log(totals)
            return 0

        lax.fori_loop(0, ROWS // 8, body, 0)

    def column_pass():
        def body(part, best):
            potentials = source_pot[pl.ds(pl.multiple_of(part * 8, 8), 8), :].T
            for inner in range(8):
                row = part * 8 + inner
                potential = potentials[:, inner : inner + 1]
                for slot in range(SLOTS):
                    block = row * SLOTS + slot
                    scores = potential - scaled[block]
                    top = jnp.max(scores, axis=0, keepdims=True)
                    total = jnp.sum(jnp.exp(scores - top), axis=0, keepdims=True)
                    peaks[pl.ds(block, 1), :] = top
                    sums[pl.ds(block, 1), :] = total
                    best = jnp.where(position == slot_at(row, slot), jnp.maximum(best, top), best)
            return best

        best = lax.fori_loop(0, ROWS // 8, body, jnp.full((GB, BLK), LOW, f32))

        def add(row, total):
            for slot in range(SLOTS):
                block = row * SLOTS + slot
                value = sums[pl.ds(block, 1), :] * jnp.exp(jnp.minimum(peaks[pl.ds(block, 1), :] - best, 0.0))
                total = total + jnp.where(position == slot_at(row, slot), value, 0.0)
            return total

        total = lax.fori_loop(0, ROWS, add, jnp.zeros((GB, BLK), f32))
        return jnp.where(total > 0.0, best + jnp.log(jnp.maximum(total, 1e-30)), LOW)

    def merge(values):
        top = functools.reduce(jnp.maximum, values)
        total = functools.reduce(jnp.add, [jnp.exp(value - top) for value in values])
        return top + jnp.log(total)

    def iteration(step):
        row_pass(step)
        copies = []
        for dx in (1, 2, 3):
            copies.append(
                remote(
                    row_lse.at[step],
                    row_land.at[step, dx - 1],
                    row_send.at[step, dx],
                    row_recv.at[step, dx],
                    device(0, 0, 0, dx),
                )
            )
            start(copies[-1])
        for copy in copies:
            copy.wait_recv()
        source_pot[...] = log_source[...] - merge([row_lse[step]] + [row_land[step, n] for n in range(3)])
        half_out[step] = column_pass()
        copy = remote(
            half_out.at[step, pl.ds(pl.multiple_of(theirs, 16), 16)],
            half_land.at[step],
            half_send.at[step],
            half_recv.at[step],
            device(0, 0, 1),
        )
        start(copy)
        copy.wait_recv()
        own = half_out[step, pl.ds(pl.multiple_of(mine, 16), 16), :]
        merged[step] = merge([own, half_land[step]])
        copies = []
        for dz in range(4):
            for dy in range(4):
                number = dz * 4 + dy
                if number:
                    copies.append(
                        remote(
                            merged.at[step],
                            merged_land.at[step, number - 1],
                            merge_send.at[step, number],
                            merge_recv.at[step, number],
                            device(dz, dy),
                        )
                    )
                    start(copies[-1])
        for copy in copies:
            copy.wait_recv()
        total = merge([merged[step]] + [merged_land[step, n] for n in range(15)])
        own = log_target[pl.ds(pl.multiple_of(mine, 16), 16), :] - total
        here = target_pot.at[step + 1, pl.ds(pl.multiple_of(mine, 16), 16)]
        here[...] = own.reshape(16, 1, BLK)
        if step < ITERS - 1:
            copy = remote(here, here, pot_send.at[step], pot_recv.at[step], device(0, 0, 1))
            start(copy)
            copy.wait_recv()

    for step in range(ITERS):
        iteration(step)
    source_out[...] = source_pot[...] * ENTROPY
    target_out[...] = target_pot[ITERS, mine + z * 4 + y] * ENTROPY
    for copy in started:
        copy.wait_send()
    out_copy.wait()


def per_device(
    coupling,
    coupling_index,
    near_cost,
    near_index,
    source_weights,
    target_cost,
    target_index,
    target_weights,
):
    smem = pl.BlockSpec(memory_space=pltpu.SMEM)
    vmem = pl.BlockSpec(memory_space=pltpu.VMEM)
    anywhere = pl.BlockSpec(memory_space=pl.ANY)
    dma = pltpu.SemaphoreType.DMA
    moves = len(PIECES)
    blocks = ROWS * SLOTS
    cost, source, target = pl.pallas_call(
        kernel,
        out_shape=(
            jax.ShapeDtypeStruct((blocks, BLK, BLK), f32),
            jax.ShapeDtypeStruct((ROWS, BLK), f32),
            jax.ShapeDtypeStruct((1, BLK), f32),
        ),
        in_specs=[smem, smem, smem, vmem, vmem, anywhere, anywhere, anywhere],
        out_specs=(anywhere, vmem, vmem),
        scratch_shapes=[
            pltpu.VMEM((ROWS * NEAR, BLK, BLK), f32),
            pltpu.VMEM((blocks, BLK, BLK), f32),
            pltpu.VMEM((ROWS, BLK, 2 * BLK), bf16),
            pltpu.VMEM((ROWS, BLK, 2 * BLK), bf16),
            pltpu.VMEM((ROWS, 2 * BLK, 6 * BLK), bf16),
            pltpu.VMEM((ROWS, BLK, BLK), f32),
            pltpu.VMEM((GB * SHARD, BLK), f32),
            pltpu.VMEM((GB * LINKS + 1, BLK, BLK), bf16),
            pltpu.VMEM((GB * LINKS + 1, BLK, BLK), bf16),
            pltpu.VMEM((blocks, BLK, BLK), f32),
            pltpu.VMEM((blocks, BLK, BLK), f32),
            pltpu.VMEM((ROWS, BLK), f32),
            pltpu.VMEM((ROWS, 1, BLK), f32),
            pltpu.VMEM((1, BLK), f32),
            pltpu.VMEM((4, 1, BLK), f32),
            pltpu.VMEM((2, 4, 4, 8, BLK), f32),
            pltpu.VMEM((GB, 1, BLK), f32),
            pltpu.VMEM((ROWS, BLK), f32),
            pltpu.VMEM((GB, BLK), f32),
            pltpu.VMEM((ITERS, ROWS, BLK), f32),
            pltpu.VMEM((ITERS, 3, ROWS, BLK), f32),
            pltpu.VMEM((ROWS, BLK), f32),
            pltpu.VMEM((ITERS, GB, BLK), f32),
            pltpu.VMEM((ITERS, 16, BLK), f32),
            pltpu.VMEM((ITERS, 16, BLK), f32),
            pltpu.VMEM((ITERS, 15, 16, BLK), f32),
            pltpu.VMEM((ITERS + 1, GB, 1, BLK), f32),
            pltpu.VMEM((blocks, BLK), f32),
            pltpu.VMEM((blocks, BLK), f32),
            dma((10,)),
            dma((moves,)),
            dma((moves,)),
            dma((moves + 1,)),
            dma((moves + 1,)),
            dma((4,)),
            dma((4,)),
            dma((7,)),
            dma((7,)),
            dma((ITERS, 4)),
            dma((ITERS, 4)),
            dma((ITERS,)),
            dma((ITERS,)),
            dma((ITERS, 16)),
            dma((ITERS, 16)),
            dma((ITERS,)),
            dma((ITERS,)),
        ],
        compiler_params=pltpu.CompilerParams(
            collective_id=0, has_side_effects=True, vmem_limit_bytes=60 * 2**20
        ),
        name="gromov_step",
    )(
        coupling_index.transpose(1, 2, 0).reshape(SLOTS, ROWS),
        near_index.T,
        target_index.transpose(2, 0, 1),
        source_weights.reshape(ROWS, BLK),
        target_weights,
        coupling.reshape(blocks, BLK, BLK),
        near_cost.reshape(ROWS * NEAR, BLK, BLK),
        target_cost.reshape(SHARD, BLK),
    )
    return (
        cost.reshape(ROWS, 1, SLOTS, BLK, BLK),
        source.reshape(ROWS * BLK),
        target,
    )


def solution(mesh):
    placed = (
        P("rows", "cols", None, None, None),
        P("rows", "cols", None),
        P("rows", None, None, None),
        P("rows", None),
        P("rows"),
        P("cols", "rows", None, None, None),
        P("cols", None, None),
        P("cols", "rows"),
    )
    return jax.shard_map(
        per_device,
        mesh=mesh,
        in_specs=placed,
        out_specs=(P("rows", "cols", None, None, None), P("rows"), P("cols", "rows")),
        check_vma=False,
    )
```

time: 1520 us -> 101 us (0.07)
  blocking collectives: 928 us -> 0 us
  other arithmetic: 259 us -> 0 us
  matrix products: 212 us -> 0 us
  Pallas kernels: 0 us -> 94.2 us
  local copies, waits for them, and re-layouts: 94.4 us -> 5.82 us
    psum x8 -> x0, blocking collectives: 478 us -> none  [the longest x3 371 us: per_device(): column_total = lax.psum(column_part, 'rows')]
    pmax x6 -> x0, blocking collectives: 426 us -> none  [the longest x3 393 us: per_device(): column_peak = lax.pmax(column_peak, 'rows')]
    dot_general x9 -> x0, matrix products: 212 us -> none  [the longest x1 99.7 us: per_device(): jnp.einsum('ikqmxz,ikqml->ilxz', through, match, precision=full_precision)]
    reduce_sum x8 -> x0, other arithmetic: 206 us -> none  [the longest x3 182 us: per_device(): jnp.sum(jnp.exp(scores - row_peak[:, None, :, None]), axis=(1, 3))]
    pallas_call x0 -> x1, Pallas kernels: none -> 94.2 us  [per_device(): pl.pallas_call(kernel, out_shape=(jax.ShapeDtypeStruct((blocks, BLK, BLK)...]
    transpose x1 -> x0, local copies, waits for them, and re-layouts: 50 us -> none  [per_device(): jnp.einsum('ikqxy,ikqmyz->ikqmxz', partial_blocks, far_blocks, precision=...]
    reduce_max x9 -> x0, other arithmetic: 45.8 us -> none  [the longest x3 22.5 us: per_device(): row_peak = jnp.max(scores, axis=(1, 3))]
    gather x14 -> x0, local copies, waits for them, and re-layouts: 37.2 us -> none  [the longest x1 20 us: per_device(): far_blocks = group_cost[far_slots]]
  transfers between devices with their start and end apart: 1 -> 0, of which waited for: 0 -> 0; matrix products, arithmetic and copies ran while one was open for 4% -> 0% of each run, Pallas kernels for 0% -> 0%
where the time goes in v1:
time: 101 us
  Pallas kernels  94.2 us (93%)
  local copies, waits for them, and re-layouts  5.82 us (6%)
    pallas_call x1, Pallas kernels, per_device(): pl.pallas_call(kernel, out_shape=(jax.ShapeDtypeStruct((blocks, BLK, BLK)...  94.2 us
    unnamed x7, local copies, waits for them, and re-layouts  5.82 us

profile of v1, /device:TPU:1, one launch (start us, length us, event | category | flops | bytes accessed | tf_op | source)
XLA Modules:
  0.0 100.6 jit_solution(5517388608058967483)
XLA Ops:
  0.6 94.2 %gromov_step.1 = (f32[64,128,128]{2,1,0:T(8,128)}, f32[32,128]{1,0:T(8,128)}, f32[1,128]{1,0:T(1,128)}) custom-call(s32[2,32]{1,0:T(2,128)} %bitcast.21, s32[3,32]{1,0:T(4,128)} %bitcast.19, s32[3,1,32]{2,1,0:T(1,128)} %bitcast.20, s32[32,128]{1,0:T(8,128)} %bitcast.17, s32[1,128]{1,0:T(1,128)} %weight_ref.1, f32[64,128,128]{2,1,0:T(8,128)} %bitcast.14, ...), custom_call_target="tpu_custom_call" | custom-call | tf_op jit(solution)/shard_map/gromov_step/pallas_call | solution.py:524
  94.8 0.0 copy-start
  94.8 0.0 copy-start.1
  94.8 4.7 %copy.15 = f32[32,1,2,128,128]{4,3,2,1,0:T(8,128)} copy(f32[32,1,2,128,128]{4,3,2,1,0:T(8,128)} %bitcast.15) | data formatting | bytes 8388608
  99.5 0.0 copy-done
  99.5 0.6 copy.16
  100.1 0.0 copy-done.1
  100.1 0.5 copy.17
Async XLA Ops:
  94.8 4.7 %copy-start = (f32[32,128]{1,0:T(8,128)S(1)}, f32[32,128]{1,0:T(8,128)}, u32[]{:S(2)}) copy-start(f32[32,128]{1,0:T(8,128)} %get-tuple-element.7) | copy-start | bytes 49156
  94.8 5.3 %copy-start.1 = (f32[1,128]{1,0:T(1,128)S(1)}, f32[1,128]{1,0:T(1,128)}, u32[]{:S(2)}) copy-start(f32[1,128]{1,0:T(1,128)} %get-tuple-element.17) | copy-start | bytes 1540

commit v2 on v1

v2 whole, which is shorter than its diff:
```python
import functools
import itertools

import jax
import jax.numpy as jnp
from jax import lax
from jax.experimental import pallas as pl
from jax.experimental.pallas import tpu as pltpu
from jax.sharding import PartitionSpec as P

MESH = pl.DeviceIdType.MESH
BLK = 128
ROWS = 32
NEAR = 3
LINKS = 3
SLOTS = 2
GB = 32
ITERS = 3
SHARD = LINKS * BLK
HALF = SHARD // 2
QUARTER = SHARD // 4
COLS = 4
ENTROPY = 0.01
LOW = -1e30
f32 = jnp.float32
bf16 = jnp.bfloat16


def gather_plan():
    pieces = []
    for half, dz, dy, part in itertools.product(range(2), range(4), range(4), range(2)):
        if dz == 0 and dy == 0:
            continue
        first_axis = dy if half == 0 else dz
        last_axis = dz if half == 0 else dy
        axis = ("z" if half == 0 else "y") if last_axis else ("y" if half == 0 else "z")
        far = last_axis if last_axis else first_axis
        side = {1: 1, 3: -1, 2: 2 * part - 1}[far]
        came = ((dz - side) % 4, dy) if axis == "z" else (dz, (dy - side) % 4)
        pieces.append((half, dz, dy, part, axis, side, came))

    def onward(piece):
        half, dz, dy, part = piece[:4]
        after = [p for p in pieces if p[0] == half and p[3] == part and p[6] == (dz, dy)]
        return max([1 + onward(p) for p in after], default=0)

    hops = {p: onward(p) for p in pieces}
    have = {(half, 0, 0, part): 0 for half in range(2) for part in range(2)}
    left = list(pieces)
    sends = []
    arrivals = []
    slot = 0
    while left:
        sends.append([])
        for link in itertools.product("yz", (1, -1)):
            ready = [
                p
                for p in left
                if (p[4], p[5]) == link and have.get((p[0],) + p[6] + (p[3],), slot + 1) <= slot
            ]
            if ready:
                best = max(ready, key=lambda p: (hops[p], -have[(p[0],) + p[6] + (p[3],)], -left.index(p)))
                left.remove(best)
                sends[-1].append(best)
                have[best[:4]] = slot + 1 + DELAY
                arrivals.append(best)
        slot += 1
    arrivals.sort(key=lambda p: have[p[:4]])
    takes = [[p for p in arrivals if have[p[:4]] == when] for when in range(slot + 1 + DELAY)]
    number = {p: n for n, p in enumerate(arrivals)}
    return number, sends, takes


DELAY = 3
NUMBER, SENDS, TAKES = gather_plan()


def split(value):
    high = value.astype(bf16)
    return high, (value - high.astype(f32)).astype(bf16)


def dot(a, b):
    return jnp.dot(a, b, preferred_element_type=f32)


def kernel(
    slots_hbm,
    near_index_hbm,
    links_hbm,
    source_hbm,
    weight_hbm,
    coupling_hbm,
    near_hbm,
    target_hbm,
    cost_hbm,
    source_out,
    target_out,
    slots,
    near,
    links,
    source_ref,
    weight_ref,
    near_cost,
    plan,
    plan_high,
    plan_low,
    partial,
    row_sum,
    gathered,
    far_high,
    far_low,
    cost,
    scaled,
    source_float,
    source_rows,
    weight_float,
    weight_land,
    extra,
    column,
    log_source,
    log_target,
    row_lse,
    row_land,
    source_pot,
    half_out,
    half_land,
    merged,
    merged_land,
    target_pot,
    peaks,
    sums,
    best_rows,
    load_sem,
    gather_send,
    gather_recv,
    pair_send,
    pair_recv,
    early_send,
    early_recv,
    extra_send,
    extra_recv,
    row_send,
    row_recv,
    half_send,
    half_recv,
    merge_send,
    merge_recv,
    pot_send,
    pot_recv,
):
    rank = lax.axis_index("rows")
    group = lax.axis_index("cols")
    z = rank // 8
    y = (rank // 2) % 4
    core = rank % 2

    def at(dz, dy, other=0):
        return (((z + dz) % 4) * 4 + (y + dy) % 4) * 2 + (core + other) % 2

    def device(dz, dy, other=0, dx=0):
        return (at(dz, dy, other), (group + dx) % COLS)

    def remote(src, dst, send, recv, where):
        return pltpu.make_async_remote_copy(
            src_ref=src, dst_ref=dst, send_sem=send, recv_sem=recv, device_id=where, device_id_type=MESH
        )

    def piece_rows(dz, dy, half, part, other=0):
        first = at(dz, dy, other) * SHARD + half * HALF + part * QUARTER
        return gathered.at[pl.ds(pl.multiple_of(first, 8), QUARTER)]

    loads = []
    chunk = ROWS // 4
    for part in range(4):
        loads.append(
            pltpu.make_async_copy(
                coupling_hbm.at[pl.ds(part * chunk * SLOTS, chunk * SLOTS)],
                plan.at[pl.ds(part * chunk * SLOTS, chunk * SLOTS)],
                load_sem.at[part],
            )
        )
    for part in range(4):
        loads.append(
            pltpu.make_async_copy(
                near_hbm.at[pl.ds(part * chunk * NEAR, chunk * NEAR)],
                near_cost.at[pl.ds(part * chunk * NEAR, chunk * NEAR)],
                load_sem.at[4 + part],
            )
        )
    small = []
    for number, (src, dst) in enumerate(
        [
            (weight_hbm, weight_ref),
            (source_hbm, source_ref),
            (near_index_hbm, near),
            (slots_hbm, slots),
            (links_hbm, links),
        ]
    ):
        small.append(pltpu.make_async_copy(src, dst, load_sem.at[10 + number]))
    own_rows = gathered.at[pl.ds(pl.multiple_of(rank * SHARD, 8), SHARD)]
    own_load = pltpu.make_async_copy(target_hbm, own_rows, load_sem.at[8])

    barrier = pltpu.get_barrier_semaphore()
    neighbours = [device(0, 0, 1), device(0, 1), device(0, 3), device(1, 0), device(3, 0)]
    neighbours += [device(0, 0, 0, dx) for dx in (1, 2, 3)]
    for where in neighbours:
        pl.semaphore_signal(barrier, inc=1, device_id=where, device_id_type=MESH)
    for copy in small + [own_load] + loads:
        copy.start()
    small[0].wait()
    weight_float[...] = weight_ref[...].astype(f32)
    pl.semaphore_wait(barrier, len(neighbours))

    started = []

    def start(copy):
        copy.start()
        started.append(copy)

    def send(piece):
        half, dz, dy, part, axis, side, came = piece
        dst = piece_rows(*came, half, part)
        if came == (0, 0):
            src = target_hbm.at[pl.ds(half * HALF + part * QUARTER, QUARTER)]
        else:
            src = dst
        number = NUMBER[piece]
        where = device(-side, 0) if axis == "z" else device(0, -side)
        start(remote(src, dst, gather_send.at[number], gather_recv.at[number], where))

    def split_rows(owner, half, part):
        first = half * HALF + part * QUARTER
        end = first + QUARTER
        while first < end:
            link = first // BLK
            size = min(end, (link + 1) * BLK) - first
            high, low = split(gathered[pl.ds(pl.multiple_of(owner * SHARD + first, 8), size), :])
            far_high[owner * LINKS + link, first - link * BLK : first - link * BLK + size, :] = high
            far_low[owner * LINKS + link, first - link * BLK : first - link * BLK + size, :] = low
            first += size

    def pair_copy(piece, other):
        here = piece_rows(piece[1], piece[2], piece[0], piece[3], other)
        number = NUMBER[piece]
        return remote(here, here, pair_send.at[number], pair_recv.at[number], device(0, 0, 1))

    def take(slot):
        pieces = TAKES[slot] if slot < len(TAKES) else []
        for piece in pieces:
            half, dz, dy, part = piece[:4]
            here = piece_rows(dz, dy, half, part)
            number = NUMBER[piece]
            remote(here, here, gather_send.at[number], gather_recv.at[number], device(0, 0, 1)).wait_recv()
            start(pair_copy(piece, 0))
        return pieces

    def use(pieces, other):
        for piece in pieces:
            if other:
                pair_copy(piece, 1).wait_recv()
            split_rows(at(piece[1], piece[2], other), piece[0], piece[3])

    def slot_at(row, slot):
        wanted = slots[slot, row]
        return lax.rem(wanted, 2) * 16 + lax.div(wanted, 2)

    def block_at(far, wanted):
        found = jnp.int32(GB * LINKS)
        for link in range(LINKS):
            found = jnp.where(links[link, 0, far] == wanted, far * LINKS + link, found)
        return found

    def split_plan(row, _):
        for q in range(SLOTS):
            high, low = split(plan[row * SLOTS + q])
            plan_high[row, :, q * BLK : (q + 1) * BLK] = high
            plan_low[row, :, q * BLK : (q + 1) * BLK] = low
        return 0

    def first_product(pair, _):
        for row in (2 * pair, 2 * pair + 1):
            total = jnp.zeros((BLK, BLK), f32)
            for k in range(NEAR):
                other = lax.rem(near[k, row], ROWS)
                block = near_cost[row * NEAR + k]
                high, low = split(block)
                high_plan = plan_high[other]
                low_plan = plan_low[other]
                both = jnp.concatenate([high, low], axis=1)
                result = dot(both, jnp.concatenate([high_plan, high_plan], axis=0)) + dot(high, low_plan)
                result_high, result_low = split(result)
                partial[row, 0:BLK, k * 2 * BLK : (k + 1) * 2 * BLK] = result_high
                partial[row, BLK : 2 * BLK, k * 2 * BLK : (k + 1) * 2 * BLK] = result_low
                total = total + block * block * source_rows[other]
            row_sum[row] = jnp.broadcast_to(jnp.sum(total, axis=1, keepdims=True), (BLK, BLK))
        return 0

    def first_rows(low, high):
        for part in range(4):
            if low <= part * chunk < high:
                loads[4 + part].wait()
        lax.fori_loop(low // 2, high // 2, first_product, 0)

    def plan_rows(part):
        loads[part].wait()
        lax.fori_loop(part * chunk, (part + 1) * chunk, split_plan, 0)

    def own_share():
        own_load.wait()
        own_weight = weight_float[...]
        weight_column = jnp.broadcast_to(own_weight, (BLK, BLK)).T
        extra_rows = [own_weight]
        for link in range(LINKS):
            block = gathered[pl.ds(pl.multiple_of(rank * SHARD + link * BLK, 8), BLK), :]
            extra_rows.append(jnp.sum(block * block * weight_column, axis=0, keepdims=True))
        across = own_weight
        for dx in (1, 2, 3):
            early(dx).wait_recv()
            across = across + weight_land[dx]
        extra_rows.append(across)
        extra_rows.append(jnp.sum(source_float[...], axis=0, keepdims=True))
        extra_rows.append(jnp.zeros((2, BLK), f32))
        extra[core, z, y] = jnp.concatenate(extra_rows, axis=0)

    def early(dx):
        return remote(
            weight_float, weight_land.at[dx], early_send.at[dx], early_recv.at[dx], device(0, 0, 0, dx)
        )

    def extra_copy(number):
        if number == 0:
            here, where = extra.at[core], device(0, 0, 1)
        elif number < 4:
            here, where = extra.at[core, z, y], device(0, number)
        else:
            here, where = extra.at[core, z], device(number - 3, 0)
        return remote(here, here, extra_send.at[number], extra_recv.at[number], where)

    pair_own = len(NUMBER)
    from_pair = []
    rows_done = 0
    for slot in range(len(TAKES) + 2):
        taken = take(slot)
        if slot < len(SENDS):
            for piece in SENDS[slot]:
                send(piece)
        if slot == 0:
            plan_rows(0)
            plan_rows(1)
            for copy in small[1:]:
                copy.wait()
            source_float[...] = source_ref[...].astype(f32)
            source_rows[...] = source_float[...].reshape(ROWS, 1, BLK)
        elif slot == 1:
            plan_rows(2)
            plan_rows(3)
            own_rows = gathered.at[pl.ds(pl.multiple_of(rank * SHARD, 8), SHARD)]
            start(remote(target_hbm, own_rows, pair_send.at[pair_own], pair_recv.at[pair_own], device(0, 0, 1)))
            for dx in (1, 2, 3):
                start(early(dx))
        elif slot == 4:
            own_share()
            for half, part in itertools.product(range(2), range(2)):
                split_rows(rank, half, part)
        elif slot == 8:
            for number in (1, 2, 3):
                start(extra_copy(number))
        elif slot == 11:
            for number in (1, 2, 3):
                extra_copy(number).wait_recv()
            for number in (4, 5, 6):
                start(extra_copy(number))
        elif slot == 15:
            for number in (4, 5, 6):
                extra_copy(number).wait_recv()
            start(extra_copy(0))
        use(taken, 0)
        from_pair.append(taken)
        if slot >= 2:
            use(from_pair[slot - 2], 1)
        if slot >= 2 and rows_done < ROWS:
            more = min(ROWS, rows_done + 4)
            first_rows(rows_done, more)
            rows_done = more
    here = gathered.at[pl.ds(pl.multiple_of(at(0, 0, 1) * SHARD, 8), SHARD)]
    remote(here, here, pair_send.at[pair_own], pair_recv.at[pair_own], device(0, 0, 1)).wait_recv()
    for half, part in itertools.product(range(2), range(2)):
        split_rows(at(0, 0, 1), half, part)
    extra_copy(0).wait_recv()
    far_high[GB * LINKS] = jnp.zeros((BLK, BLK), bf16)
    far_low[GB * LINKS] = jnp.zeros((BLK, BLK), bf16)

    everything = extra[...].reshape(GB, 8, BLK)
    target_total = jnp.sum(everything[:, 4, :])
    source_total = jnp.sum(everything[:, 5, :])
    target_scale = (COLS * GB * BLK) / target_total
    source_scale = (GB * ROWS * BLK) / source_total
    log_source[...] = jnp.log(source_float[...] * source_scale)
    log_target[...] = jnp.log(everything[:, 0, :] * target_scale)
    column_scale = target_scale / (LINKS * BLK)
    row_scale = source_scale / (NEAR * BLK)
    position = lax.broadcasted_iota(jnp.int32, (GB, BLK), 0)

    def add_column(step, total):
        own = (step % 16) * 2 + step // 16
        for link in range(LINKS):
            lands = links[link, 0, own]
            lands = lax.rem(lands, 2) * 16 + lax.div(lands, 2)
            value = extra[step // 16, (step // 4) % 4, step % 4, 1 + link : 2 + link, :]
            total = total + jnp.where(position == lands, value, 0.0)
        return total

    column_term = lax.fori_loop(0, GB, add_column, jnp.zeros((GB, BLK), f32)) * column_scale
    column[...] = column_term.reshape(GB, 1, BLK)

    factor = 2.0 / (NEAR * BLK) / (COLS * SLOTS * BLK)

    def second_row(row):
        high_rows = []
        low_rows = []
        wanted = [slots[slot, row] for slot in range(SLOTS)]
        for k in range(NEAR):
            other = lax.rem(near[k, row], ROWS)
            for q in range(SLOTS):
                far = slots[q, other]
                found = [block_at(far, wanted[slot]) for slot in range(SLOTS)]
                high_rows.append(jnp.concatenate([far_high[n] for n in found], axis=1))
                low_rows.append(jnp.concatenate([far_low[n] for n in found], axis=1))
        result = dot(partial[row], jnp.concatenate(high_rows, axis=0))
        result = result[0:BLK] + result[BLK : 2 * BLK]
        result = result + dot(partial[row, 0:BLK, :], jnp.concatenate(low_rows, axis=0))
        across = row_sum[row] * row_scale
        scores = []
        for slot in range(SLOTS):
            own_column = column[slot_at(row, slot)]
            value = across + own_column - factor * result[:, slot * BLK : (slot + 1) * BLK]
            cost[row * SLOTS + slot] = value
            value = value * (1.0 / ENTROPY)
            scaled[row * SLOTS + slot] = value
            scores.append(-value)
        return scores

    def row_sums(scores):
        top = jnp.max(jnp.maximum(scores[0], scores[1]), axis=1, keepdims=True)
        total = jnp.sum(jnp.exp(scores[0] - top) + jnp.exp(scores[1] - top), axis=1, keepdims=True)
        return top, total

    def row_result(found):
        tops = jnp.concatenate([top for top, _ in found], axis=1).T
        totals = jnp.concatenate([total for _, total in found], axis=1).T
        return tops + jnp.log(totals)

    def second_product(part, _):
        found = [row_sums(second_row(part * 4 + inner)) for inner in range(4)]
        row_lse[0, pl.ds(pl.multiple_of(part * 4, 4), 4), :] = row_result(found)
        return 0

    lax.fori_loop(0, ROWS // 4, second_product, 0)
    out_copy = pltpu.make_async_copy(cost, cost_hbm, load_sem.at[9])
    out_copy.start()

    mine = core * 16
    theirs = 16 - mine
    part_rows = ROWS // 2

    def row_pass(step, part):
        found = []
        for row in range(part * part_rows, (part + 1) * part_rows):
            found.append(
                row_sums(
                    [
                        target_pot[step, slot_at(row, slot)] - scaled[row * SLOTS + slot]
                        for slot in range(SLOTS)
                    ]
                )
            )
        row_lse[step, part * part_rows : (part + 1) * part_rows, :] = row_result(found)

    def column_pass(part, best):
        potentials = source_pot[part * part_rows : (part + 1) * part_rows, :].T
        for inner in range(part_rows):
            row = part * part_rows + inner
            potential = potentials[:, inner : inner + 1]
            for slot in range(SLOTS):
                block = row * SLOTS + slot
                scores = potential - scaled[block]
                top = jnp.max(scores, axis=0, keepdims=True)
                total = jnp.sum(jnp.exp(scores - top), axis=0, keepdims=True)
                peaks[block : block + 1, :] = top
                sums[block : block + 1, :] = total
                best = jnp.where(position == slot_at(row, slot), jnp.maximum(best, top), best)
        return best

    def column_result(best):
        best_rows[...] = best.reshape(GB, 1, BLK)
        every = [(row, slot) for row in range(ROWS) for slot in range(SLOTS)]
        tops = jnp.concatenate([best_rows[slot_at(row, slot)] for row, slot in every], axis=0)
        values = sums[...] * jnp.exp(peaks[...] - tops)
        total = jnp.zeros((GB, BLK), f32)
        for block, (row, slot) in enumerate(every):
            total = total + jnp.where(position == slot_at(row, slot), values[block : block + 1, :], 0.0)
        return jnp.where(total > 0.0, best + jnp.log(jnp.maximum(total, 1e-30)), LOW)

    def merge(values):
        top = functools.reduce(jnp.maximum, values)
        total = functools.reduce(jnp.add, [jnp.exp(value - top) for value in values])
        return top + jnp.log(total)

    def iteration(step, _):
        moved = []

        def move(copy):
            copy.start()
            moved.append(copy)
            return copy

        row_copies = []
        for part in range(2):
            pl.when(step > 0)(functools.partial(row_pass, step, part))
            rows = pl.ds(part * part_rows, part_rows)
            row_copies.append(
                [
                    move(
                        remote(
                            row_lse.at[step, rows],
                            row_land.at[step, dx - 1, rows],
                            row_send.at[step, part, dx],
                            row_recv.at[step, part, dx],
                            device(0, 0, 0, dx),
                        )
                    )
                    for dx in (1, 2, 3)
                ]
            )
        best = jnp.full((GB, BLK), LOW, f32)
        for part in range(2):
            for copy in row_copies[part]:
                copy.wait_recv()
            rows = slice(part * part_rows, (part + 1) * part_rows)
            arrived = [row_lse[step, rows, :]] + [row_land[step, n, rows, :] for n in range(3)]
            source_pot[rows, :] = log_source[rows, :] - merge(arrived)
            best = column_pass(part, best)
        half_out[step] = column_result(best)
        move(
            remote(
                half_out.at[step, pl.ds(pl.multiple_of(theirs, 16), 16)],
                half_land.at[step],
                half_send.at[step],
                half_recv.at[step],
                device(0, 0, 1),
            )
        ).wait_recv()
        own = half_out[step, pl.ds(pl.multiple_of(mine, 16), 16), :]
        merged[step] = merge([own, half_land[step]])
        copies = []
        for number in range(1, 16):
            copies.append(
                move(
                    remote(
                        merged.at[step],
                        merged_land.at[step, number - 1],
                        merge_send.at[step, number],
                        merge_recv.at[step, number],
                        device(number // 4, number % 4),
                    )
                )
            )
        for copy in copies:
            copy.wait_recv()
        total = merge([merged[step]] + [merged_land[step, n] for n in range(15)])
        own = log_target[pl.ds(pl.multiple_of(mine, 16), 16), :] - total
        here = target_pot.at[step + 1, pl.ds(pl.multiple_of(mine, 16), 16)]
        here[...] = own.reshape(16, 1, BLK)

        @pl.when(step < ITERS - 1)
        def _():
            copy = remote(here, here, pot_send.at[step], pot_recv.at[step], device(0, 0, 1))
            copy.start()
            copy.wait_recv()
            copy.wait_send()

        for copy in moved:
            copy.wait_send()
        return 0

    lax.fori_loop(0, ITERS, iteration, 0)
    source_out[...] = source_pot[...] * ENTROPY
    target_out[...] = target_pot[ITERS, mine + z * 4 + y] * ENTROPY
    for copy in started:
        copy.wait_send()
    out_copy.wait()


def hand_over(cost, source, target, cost_out, source_out, target_out, held, load, store):
    parts = 4
    size = held.shape[0] // parts
    refs = [(cost.at[pl.ds(n * size, size)], held.at[pl.ds(n * size, size)]) for n in range(parts)]
    loads = [pltpu.make_async_copy(src, dst, load.at[n]) for n, (src, dst) in enumerate(refs)]
    for copy in loads:
        copy.start()
    source_out[...] = source[...]
    target_out[...] = target[...]
    stores = []
    for n in range(parts):
        loads[n].wait()
        dst = cost_out.at[pl.ds(n * size, size)]
        stores.append(pltpu.make_async_copy(refs[n][1], dst, store.at[n]))
        stores[-1].start()
    for copy in stores:
        copy.wait()


def per_device(
    coupling,
    coupling_index,
    near_cost,
    near_index,
    source_weights,
    target_cost,
    target_index,
    target_weights,
):
    vmem = pl.BlockSpec(memory_space=pltpu.VMEM)
    anywhere = pl.BlockSpec(memory_space=pl.ANY)
    dma = pltpu.SemaphoreType.DMA
    moves = len(NUMBER)
    blocks = ROWS * SLOTS
    cost, source, target = pl.pallas_call(
        kernel,
        out_shape=(
            jax.ShapeDtypeStruct((blocks, BLK, BLK), f32),
            jax.ShapeDtypeStruct((ROWS, BLK), f32),
            jax.ShapeDtypeStruct((1, BLK), f32),
        ),
        in_specs=[anywhere] * 8,
        out_specs=(anywhere, vmem, vmem),
        scratch_shapes=[
            pltpu.SMEM((SLOTS, ROWS), jnp.int32),
            pltpu.SMEM((NEAR, ROWS), jnp.int32),
            pltpu.SMEM((LINKS, 1, GB), jnp.int32),
            pltpu.VMEM((ROWS, BLK), jnp.int32),
            pltpu.VMEM((1, BLK), jnp.int32),
            pltpu.VMEM((ROWS * NEAR, BLK, BLK), f32),
            pltpu.VMEM((blocks, BLK, BLK), f32),
            pltpu.VMEM((ROWS, BLK, 2 * BLK), bf16),
            pltpu.VMEM((ROWS, BLK, 2 * BLK), bf16),
            pltpu.VMEM((ROWS, 2 * BLK, 6 * BLK), bf16),
            pltpu.VMEM((ROWS, BLK, BLK), f32),
            pltpu.VMEM((GB * SHARD, BLK), f32),
            pltpu.VMEM((GB * LINKS + 1, BLK, BLK), bf16),
            pltpu.VMEM((GB * LINKS + 1, BLK, BLK), bf16),
            pltpu.VMEM((blocks, BLK, BLK), f32),
            pltpu.VMEM((blocks, BLK, BLK), f32),
            pltpu.VMEM((ROWS, BLK), f32),
            pltpu.VMEM((ROWS, 1, BLK), f32),
            pltpu.VMEM((1, BLK), f32),
            pltpu.VMEM((4, 1, BLK), f32),
            pltpu.VMEM((2, 4, 4, 8, BLK), f32),
            pltpu.VMEM((GB, 1, BLK), f32),
            pltpu.VMEM((ROWS, BLK), f32),
            pltpu.VMEM((GB, BLK), f32),
            pltpu.VMEM((ITERS, ROWS, BLK), f32),
            pltpu.VMEM((ITERS, 3, ROWS, BLK), f32),
            pltpu.VMEM((ROWS, BLK), f32),
            pltpu.VMEM((ITERS, GB, BLK), f32),
            pltpu.VMEM((ITERS, 16, BLK), f32),
            pltpu.VMEM((ITERS, 16, BLK), f32),
            pltpu.VMEM((ITERS, 15, 16, BLK), f32),
            pltpu.VMEM((ITERS + 1, GB, 1, BLK), f32),
            pltpu.VMEM((blocks, BLK), f32),
            pltpu.VMEM((blocks, BLK), f32),
            pltpu.VMEM((GB, 1, BLK), f32),
            dma((15,)),
            dma((moves,)),
            dma((moves,)),
            dma((moves + 1,)),
            dma((moves + 1,)),
            dma((4,)),
            dma((4,)),
            dma((7,)),
            dma((7,)),
            dma((ITERS, 2, 4)),
            dma((ITERS, 2, 4)),
            dma((ITERS,)),
            dma((ITERS,)),
            dma((ITERS, 16)),
            dma((ITERS, 16)),
            dma((ITERS,)),
            dma((ITERS,)),
        ],
        compiler_params=pltpu.CompilerParams(
            collective_id=0, has_side_effects=True, vmem_limit_bytes=60 * 2**20
        ),
        name="gromov_step",
    )(
        coupling_index.transpose(1, 2, 0).reshape(SLOTS, ROWS),
        near_index.T,
        target_index.transpose(2, 0, 1),
        source_weights.reshape(ROWS, BLK),
        target_weights,
        coupling.reshape(blocks, BLK, BLK),
        near_cost.reshape(ROWS * NEAR, BLK, BLK),
        target_cost.reshape(SHARD, BLK),
    )
    cost, source, target = pl.pallas_call(
        hand_over,
        out_shape=tuple(jax.ShapeDtypeStruct(x.shape, x.dtype) for x in (cost, source, target)),
        in_specs=[anywhere, vmem, vmem],
        out_specs=(anywhere, vmem, vmem),
        scratch_shapes=[pltpu.VMEM((blocks, BLK, BLK), f32), dma((4,)), dma((4,))],
        compiler_params=pltpu.CompilerParams(vmem_limit_bytes=60 * 2**20),
        name="hand_over",
    )(cost, source, target)
    return (
        cost.reshape(ROWS, 1, SLOTS, BLK, BLK),
        source.reshape(ROWS * BLK),
        target,
    )


def solution(mesh):
    placed = (
        P("rows", "cols", None, None, None),
        P("rows", "cols", None),
        P("rows", None, None, None),
        P("rows", None),
        P("rows"),
        P("cols", "rows", None, None, None),
        P("cols", None, None),
        P("cols", "rows"),
    )
    return jax.shard_map(
        per_device,
        mesh=mesh,
        in_specs=placed,
        out_specs=(P("rows", "cols", None, None, None), P("rows"), P("cols", "rows")),
        check_vma=False,
    )
```

time: 101 us -> 86.1 us (0.85)
  Pallas kernels: 94.2 us -> 85.3 us
  local copies, waits for them, and re-layouts: 5.82 us -> 0 us
    pallas_call x1, Pallas kernels: 94.2 us -> 80.6 us  [per_device(): pl.pallas_call(kernel, out_shape=(jax.ShapeDtypeStruct((blocks, BLK, BLK)...]
    unnamed x7 -> x0, local copies, waits for them, and re-layouts: 5.82 us -> none
    pallas_call x0 -> x1, Pallas kernels: none -> 4.63 us  [per_device(): pl.pallas_call(hand_over, out_shape=tuple((jax.ShapeDtypeStruct(x.shape,...]
where the time goes in v2:
time: 86.1 us; the launch traced here: 85.9 us
  Pallas kernels  85.3 us (99%)
    pallas_call x1, Pallas kernels, per_device(): pl.pallas_call(kernel, out_shape=(jax.ShapeDtypeStruct((blocks, BLK, BLK)...  80.6 us
    pallas_call x1, Pallas kernels, per_device(): pl.pallas_call(hand_over, out_shape=tuple((jax.ShapeDtypeStruct(x.shape,...  4.63 us

profile of v2, /device:TPU:1, one launch (start us, length us, event | category | flops | bytes accessed | tf_op | source)
XLA Modules:
  0.0 85.9 jit_solution(8655644661708325729)
XLA Ops:
  0.6 80.6 %gromov_step.1 = (f32[64,128,128]{2,1,0:T(8,128)}, f32[32,128]{1,0:T(8,128)}, f32[1,128]{1,0:T(1,128)}) custom-call(s32[2,32]{1,0:T(2,128)} %bitcast.19, s32[3,32]{1,0:T(4,128)} %bitcast.17, s32[3,1,32]{2,1,0:T(1,128)} %bitcast.18, s32[32,128]{1,0:T(8,128)} %bitcast.16, s32[1,128]{1,0:T(1,128)} %weight_hbm.1, f32[64,128,128]{2,1,0:T(8,128)} %bitcast.14, ...), custom_call_target="tpu_custom_call" | custom-call | tf_op jit(solution)/shard_map/gromov_step/pallas_call | solution.py:630
  81.3 4.6 %hand_over.1 = (f32[64,128,128]{2,1,0:T(8,128)}, f32[32,128]{1,0:T(8,128)}, f32[1,128]{1,0:T(1,128)}) custom-call(f32[64,128,128]{2,1,0:T(8,128)} %get-tuple-element.9.cost, f32[32,128]{1,0:T(8,128)} %get-tuple-element.10.source, f32[1,128]{1,0:T(1,128)} %get-tuple-element.11.target), custom_call_target="tpu_custom_call" | custom-call | tf_op jit(solution)/shard_map/hand_over/pallas_call | solution.py:707

commit v3 on v2

--- a/solution.py
+++ b/solution.py
@@ -72,6 +72,7 @@
 
 
 DELAY = 3
+FARTHEST_FIRST = sorted(range(1, 16), key=lambda n: abs(n // 4 - 2) + abs(n % 4 - 2))
 NUMBER, SENDS, TAKES = gather_plan()
 
 
@@ -110,8 +111,6 @@
     gathered,
     far_high,
     far_low,
-    cost,
-    scaled,
     source_float,
     source_rows,
     weight_float,
@@ -149,6 +148,9 @@
     pot_send,
     pot_recv,
 ):
+    cost = plan
+    scaled = near_cost
+
     rank = lax.axis_index("rows")
     group = lax.axis_index("cols")
     z = rank // 8
@@ -204,7 +206,7 @@
 
     barrier = pltpu.get_barrier_semaphore()
     neighbours = [device(0, 0, 1), device(0, 1), device(0, 3), device(1, 0), device(3, 0)]
-    neighbours += [device(0, 0, 0, dx) for dx in (1, 2, 3)]
+    neighbours += [device(0, 0, 0, dx) for dx in (1, 3)]
     for where in neighbours:
         pl.semaphore_signal(barrier, inc=1, device_id=where, device_id_type=MESH)
     for copy in small + [own_load] + loads:
@@ -316,8 +318,9 @@
             block = gathered[pl.ds(pl.multiple_of(rank * SHARD + link * BLK, 8), BLK), :]
             extra_rows.append(jnp.sum(block * block * weight_column, axis=0, keepdims=True))
         across = own_weight
+        for dx in (3, 2):
+            early(dx).wait_recv()
         for dx in (1, 2, 3):
-            early(dx).wait_recv()
             across = across + weight_land[dx]
         extra_rows.append(across)
         extra_rows.append(jnp.sum(source_float[...], axis=0, keepdims=True))
@@ -325,9 +328,9 @@
         extra[core, z, y] = jnp.concatenate(extra_rows, axis=0)
 
     def early(dx):
-        return remote(
-            weight_float, weight_land.at[dx], early_send.at[dx], early_recv.at[dx], device(0, 0, 0, dx)
-        )
+        src = weight_land.at[1] if dx == 2 else weight_float
+        where = device(0, 0, 0, 1 if dx == 2 else dx)
+        return remote(src, weight_land.at[dx], early_send.at[dx], early_recv.at[dx], where)
 
     def extra_copy(number):
         if number == 0:
@@ -358,9 +361,12 @@
             plan_rows(3)
             own_rows = gathered.at[pl.ds(pl.multiple_of(rank * SHARD, 8), SHARD)]
             start(remote(target_hbm, own_rows, pair_send.at[pair_own], pair_recv.at[pair_own], device(0, 0, 1)))
-            for dx in (1, 2, 3):
-                start(early(dx))
+            start(early(1))
+            start(early(3))
         elif slot == 4:
+            early(1).wait_recv()
+            start(early(2))
+        elif slot == 6:
             own_share()
             for half, part in itertools.product(range(2), range(2)):
                 split_rows(rank, half, part)
@@ -531,7 +537,7 @@
                             device(0, 0, 0, dx),
                         )
                     )
-                    for dx in (1, 2, 3)
+                    for dx in (2, 1, 3)
                 ]
             )
         best = jnp.full((GB, BLK), LOW, f32)
@@ -555,7 +561,7 @@
         own = half_out[step, pl.ds(pl.multiple_of(mine, 16), 16), :]
         merged[step] = merge([own, half_land[step]])
         copies = []
-        for number in range(1, 16):
+        for number in FARTHEST_FIRST:
             copies.append(
                 move(
                     remote(
@@ -593,21 +599,19 @@
     out_copy.wait()
 
 
-def hand_over(cost, source, target, cost_out, source_out, target_out, held, load, store):
+def hand_over(cost, source, target, cost_out, source_out, target_out, held, source_held, target_held, load, store):
     parts = 4
     size = held.shape[0] // parts
-    refs = [(cost.at[pl.ds(n * size, size)], held.at[pl.ds(n * size, size)]) for n in range(parts)]
-    loads = [pltpu.make_async_copy(src, dst, load.at[n]) for n, (src, dst) in enumerate(refs)]
+    rows = [pl.ds(n * size, size) for n in range(parts)]
+    steps = [(cost.at[r], held.at[r], cost_out.at[r]) for r in rows]
+    steps[1:1] = [(source, source_held, source_out), (target, target_held, target_out)]
+    loads = [pltpu.make_async_copy(src, here, load.at[n]) for n, (src, here, _) in enumerate(steps)]
+    stores = [pltpu.make_async_copy(here, dst, store.at[n]) for n, (_, here, dst) in enumerate(steps)]
     for copy in loads:
         copy.start()
-    source_out[...] = source[...]
-    target_out[...] = target[...]
-    stores = []
-    for n in range(parts):
-        loads[n].wait()
-        dst = cost_out.at[pl.ds(n * size, size)]
-        stores.append(pltpu.make_async_copy(refs[n][1], dst, store.at[n]))
-        stores[-1].start()
+    for came, goes in zip(loads, stores):
+        came.wait()
+        goes.start()
     for copy in stores:
         copy.wait()
 
@@ -651,8 +655,6 @@
             pltpu.VMEM((GB * SHARD, BLK), f32),
             pltpu.VMEM((GB * LINKS + 1, BLK, BLK), bf16),
             pltpu.VMEM((GB * LINKS + 1, BLK, BLK), bf16),
-            pltpu.VMEM((blocks, BLK, BLK), f32),
-            pltpu.VMEM((blocks, BLK, BLK), f32),
             pltpu.VMEM((ROWS, BLK), f32),
             pltpu.VMEM((ROWS, 1, BLK), f32),
             pltpu.VMEM((1, BLK), f32),
@@ -707,9 +709,15 @@
     cost, source, target = pl.pallas_call(
         hand_over,
         out_shape=tuple(jax.ShapeDtypeStruct(x.shape, x.dtype) for x in (cost, source, target)),
-        in_specs=[anywhere, vmem, vmem],
-        out_specs=(anywhere, vmem, vmem),
-        scratch_shapes=[pltpu.VMEM((blocks, BLK, BLK), f32), dma((4,)), dma((4,))],
+        in_specs=[anywhere] * 3,
+        out_specs=(anywhere,) * 3,
+        scratch_shapes=[
+            pltpu.VMEM((blocks, BLK, BLK), f32),
+            pltpu.VMEM((ROWS, BLK), f32),
+            pltpu.VMEM((1, BLK), f32),
+            dma((6,)),
+            dma((6,)),
+        ],
         compiler_params=pltpu.CompilerParams(vmem_limit_bytes=60 * 2**20),
         name="hand_over",
     )(cost, source, target)

time: 86.1 us -> 83.6 us (0.971)
  Pallas kernels: 85.3 us -> 82.9 us
    pallas_call x1, Pallas kernels: 4.63 us -> 3.36 us  [per_device(): pl.pallas_call(hand_over, out_shape=tuple((jax.ShapeDtypeStruct(x.shape,...]
    pallas_call x1, Pallas kernels: 80.6 us -> 79.5 us  [per_device(): pl.pallas_call(kernel, out_shape=(jax.ShapeDtypeStruct((blocks, BLK, BLK)...]
where the time goes in v3:
time: 83.6 us; the launch traced here: 83.5 us
  Pallas kernels  82.9 us (99%)
    pallas_call x1, Pallas kernels, per_device(): pl.pallas_call(kernel, out_shape=(jax.ShapeDtypeStruct((blocks, BLK, BLK)...  79.5 us
    pallas_call x1, Pallas kernels, per_device(): pl.pallas_call(hand_over, out_shape=tuple((jax.ShapeDtypeStruct(x.shape,...  3.36 us

profile of v3, /device:TPU:1, one launch (start us, length us, event | category | flops | bytes accessed | tf_op | source)
XLA Modules:
  0.0 83.5 jit_solution(16325789751960166285)
XLA Ops:
  0.6 79.5 %gromov_step.1 = (f32[64,128,128]{2,1,0:T(8,128)}, f32[32,128]{1,0:T(8,128)}, f32[1,128]{1,0:T(1,128)}) custom-call(s32[2,32]{1,0:T(2,128)} %bitcast.19, s32[3,32]{1,0:T(4,128)} %bitcast.17, s32[3,1,32]{2,1,0:T(1,128)} %bitcast.18, s32[32,128]{1,0:T(8,128)} %bitcast.16, s32[1,128]{1,0:T(1,128)} %weight_hbm.1, f32[64,128,128]{2,1,0:T(8,128)} %bitcast.14, ...), custom_call_target="tpu_custom_call" | custom-call | tf_op jit(solution)/shard_map/gromov_step/pallas_call | solution.py:634
  80.1 3.4 %hand_over.1 = (f32[64,128,128]{2,1,0:T(8,128)}, f32[32,128]{1,0:T(8,128)}, f32[1,128]{1,0:T(1,128)}) custom-call(f32[64,128,128]{2,1,0:T(8,128)} %get-tuple-element.9.cost, f32[32,128]{1,0:T(8,128)} %get-tuple-element.10.source, f32[1,128]{1,0:T(1,128)} %get-tuple-element.11.target), custom_call_target="tpu_custom_call" | custom-call | tf_op jit(solution)/shard_map/hand_over/pallas_call | solution.py:709

commit v4 on v3

--- a/solution.py
+++ b/solution.py
@@ -72,6 +72,7 @@
 
 
 DELAY = 3
+PARTS = 4
 FARTHEST_FIRST = sorted(range(1, 16), key=lambda n: abs(n // 4 - 2) + abs(n % 4 - 2))
 NUMBER, SENDS, TAKES = gather_plan()
 
@@ -341,6 +342,33 @@
             here, where = extra.at[core, z], device(number - 3, 0)
         return remote(here, here, extra_send.at[number], extra_recv.at[number], where)
 
+    position = lax.broadcasted_iota(jnp.int32, (GB, BLK), 0)
+    row_scale_at = []
+
+    def masses():
+        everything = extra[...].reshape(GB, 8, BLK)
+        target_total = jnp.sum(everything[:, 4, :])
+        source_total = jnp.sum(everything[:, 5, :])
+        target_scale = (COLS * GB * BLK) / target_total
+        source_scale = (GB * ROWS * BLK) / source_total
+        log_source[...] = jnp.log(source_float[...] * source_scale)
+        log_target[...] = jnp.log(everything[:, 0, :] * target_scale)
+        column_scale = target_scale / (LINKS * BLK)
+        row_scale = source_scale / (NEAR * BLK)
+
+        def add_column(step, total):
+            own = (step % 16) * 2 + step // 16
+            for link in range(LINKS):
+                lands = links[link, 0, own]
+                lands = lax.rem(lands, 2) * 16 + lax.div(lands, 2)
+                value = extra[step // 16, (step // 4) % 4, step % 4, 1 + link : 2 + link, :]
+                total = total + jnp.where(position == lands, value, 0.0)
+            return total
+
+        column_term = lax.fori_loop(0, GB, add_column, jnp.zeros((GB, BLK), f32), unroll=4) * column_scale
+        column[...] = column_term.reshape(GB, 1, BLK)
+        row_scale_at.append(row_scale)
+
     pair_own = len(NUMBER)
     from_pair = []
     rows_done = 0
@@ -395,31 +423,9 @@
     for half, part in itertools.product(range(2), range(2)):
         split_rows(at(0, 0, 1), half, part)
     extra_copy(0).wait_recv()
+    masses()
     far_high[GB * LINKS] = jnp.zeros((BLK, BLK), bf16)
     far_low[GB * LINKS] = jnp.zeros((BLK, BLK), bf16)
-
-    everything = extra[...].reshape(GB, 8, BLK)
-    target_total = jnp.sum(everything[:, 4, :])
-    source_total = jnp.sum(everything[:, 5, :])
-    target_scale = (COLS * GB * BLK) / target_total
-    source_scale = (GB * ROWS * BLK) / source_total
-    log_source[...] = jnp.log(source_float[...] * source_scale)
-    log_target[...] = jnp.log(everything[:, 0, :] * target_scale)
-    column_scale = target_scale / (LINKS * BLK)
-    row_scale = source_scale / (NEAR * BLK)
-    position = lax.broadcasted_iota(jnp.int32, (GB, BLK), 0)
-
-    def add_column(step, total):
-        own = (step % 16) * 2 + step // 16
-        for link in range(LINKS):
-            lands = links[link, 0, own]
-            lands = lax.rem(lands, 2) * 16 + lax.div(lands, 2)
-            value = extra[step // 16, (step // 4) % 4, step % 4, 1 + link : 2 + link, :]
-            total = total + jnp.where(position == lands, value, 0.0)
-        return total
-
-    column_term = lax.fori_loop(0, GB, add_column, jnp.zeros((GB, BLK), f32)) * column_scale
-    column[...] = column_term.reshape(GB, 1, BLK)
 
     factor = 2.0 / (NEAR * BLK) / (COLS * SLOTS * BLK)
 
@@ -437,7 +443,7 @@
         result = dot(partial[row], jnp.concatenate(high_rows, axis=0))
         result = result[0:BLK] + result[BLK : 2 * BLK]
         result = result + dot(partial[row, 0:BLK, :], jnp.concatenate(low_rows, axis=0))
-        across = row_sum[row] * row_scale
+        across = row_sum[row] * row_scale_at[0]
         scores = []
         for slot in range(SLOTS):
             own_column = column[slot_at(row, slot)]
@@ -458,19 +464,33 @@
         totals = jnp.concatenate([total for _, total in found], axis=1).T
         return tops + jnp.log(totals)
 
+    part_rows = ROWS // PARTS
+
+    def row_copy(step, part, dx):
+        rows = pl.ds(pl.multiple_of(part * part_rows, part_rows), part_rows)
+        return remote(
+            row_lse.at[step, rows],
+            row_land.at[step, dx - 1, rows],
+            row_send.at[step, part, dx],
+            row_recv.at[step, part, dx],
+            device(0, 0, 0, dx),
+        )
+
+    def send_rows(step, part, found):
+        row_lse[step, pl.ds(pl.multiple_of(part * part_rows, part_rows), part_rows), :] = row_result(found)
+        for dx in (2, 1, 3):
+            row_copy(step, part, dx).start()
+
     def second_product(part, _):
-        found = [row_sums(second_row(part * 4 + inner)) for inner in range(4)]
-        row_lse[0, pl.ds(pl.multiple_of(part * 4, 4), 4), :] = row_result(found)
+        send_rows(0, part, [row_sums(second_row(part * part_rows + inner)) for inner in range(part_rows)])
         return 0
 
-    lax.fori_loop(0, ROWS // 4, second_product, 0)
+    lax.fori_loop(0, PARTS, second_product, 0)
     out_copy = pltpu.make_async_copy(cost, cost_hbm, load_sem.at[9])
     out_copy.start()
 
     mine = core * 16
     theirs = 16 - mine
-    part_rows = ROWS // 2
-
     def row_pass(step, part):
         found = []
         for row in range(part * part_rows, (part + 1) * part_rows):
@@ -482,7 +502,7 @@
                     ]
                 )
             )
-        row_lse[step, part * part_rows : (part + 1) * part_rows, :] = row_result(found)
+        send_rows(step, part, found)
 
     def column_pass(part, best):
         potentials = source_pot[part * part_rows : (part + 1) * part_rows, :].T
@@ -522,28 +542,12 @@
             moved.append(copy)
             return copy
 
-        row_copies = []
-        for part in range(2):
+        for part in range(PARTS):
             pl.when(step > 0)(functools.partial(row_pass, step, part))
-            rows = pl.ds(part * part_rows, part_rows)
-            row_copies.append(
-                [
-                    move(
-                        remote(
-                            row_lse.at[step, rows],
-                            row_land.at[step, dx - 1, rows],
-                            row_send.at[step, part, dx],
-                            row_recv.at[step, part, dx],
-                            device(0, 0, 0, dx),
-                        )
-                    )
-                    for dx in (2, 1, 3)
-                ]
-            )
         best = jnp.full((GB, BLK), LOW, f32)
-        for part in range(2):
-            for copy in row_copies[part]:
-                copy.wait_recv()
+        for part in range(PARTS):
+            for dx in (1, 3, 2):
+                row_copy(step, part, dx).wait_recv()
             rows = slice(part * part_rows, (part + 1) * part_rows)
             arrived = [row_lse[step, rows, :]] + [row_land[step, n, rows, :] for n in range(3)]
             source_pot[rows, :] = log_source[rows, :] - merge(arrived)
@@ -560,40 +564,59 @@
         ).wait_recv()
         own = half_out[step, pl.ds(pl.multiple_of(mine, 16), 16), :]
         merged[step] = merge([own, half_land[step]])
-        copies = []
-        for number in FARTHEST_FIRST:
-            copies.append(
-                move(
+        row_sent = [row_copy(step, part, dx) for part in range(PARTS) for dx in (1, 2, 3)]
+
+        def exchange(pieces):
+            copies = []
+            for number in FARTHEST_FIRST:
+                src, dst = pieces(number)
+                copies.append(
                     remote(
-                        merged.at[step],
-                        merged_land.at[step, number - 1],
+                        src,
+                        dst,
                         merge_send.at[step, number],
                         merge_recv.at[step, number],
                         device(number // 4, number % 4),
                     )
                 )
-            )
-        for copy in copies:
-            copy.wait_recv()
-        total = merge([merged[step]] + [merged_land[step, n] for n in range(15)])
-        own = log_target[pl.ds(pl.multiple_of(mine, 16), 16), :] - total
-        here = target_pot.at[step + 1, pl.ds(pl.multiple_of(mine, 16), 16)]
-        here[...] = own.reshape(16, 1, BLK)
+                copies[-1].start()
+            for copy in copies:
+                copy.wait_recv()
+            for copy in copies:
+                copy.wait_send()
 
         @pl.when(step < ITERS - 1)
         def _():
+            exchange(lambda number: (merged.at[step], merged_land.at[step, number - 1]))
+            total = merge([merged[step]] + [merged_land[step, n] for n in range(15)])
+            own = log_target[pl.ds(pl.multiple_of(mine, 16), 16), :] - total
+            here = target_pot.at[step + 1, pl.ds(pl.multiple_of(mine, 16), 16)]
+            here[...] = own.reshape(16, 1, BLK)
             copy = remote(here, here, pot_send.at[step], pot_recv.at[step], device(0, 0, 1))
             copy.start()
             copy.wait_recv()
             copy.wait_send()
 
+        @pl.when(step == ITERS - 1)
+        def _():
+            def pieces(number):
+                theirs_at = ((z + number // 4) % 4) * 4 + (y + number % 4) % 4
+                return merged.at[step, pl.ds(theirs_at, 1)], merged_land.at[step, number - 1, pl.ds(0, 1)]
+
+            exchange(pieces)
+            own = z * 4 + y
+            arrived = [merged_land[step, n, 0:1, :] for n in range(15)]
+            total = merge([merged[step, pl.ds(own, 1), :]] + arrived)
+            target_out[...] = (log_target[pl.ds(mine + own, 1), :] - total) * ENTROPY
+
+        for copy in row_sent:
+            copy.wait_send()
         for copy in moved:
             copy.wait_send()
         return 0
 
     lax.fori_loop(0, ITERS, iteration, 0)
     source_out[...] = source_pot[...] * ENTROPY
-    target_out[...] = target_pot[ITERS, mine + z * 4 + y] * ENTROPY
     for copy in started:
         copy.wait_send()
     out_copy.wait()
@@ -683,8 +706,8 @@
             dma((4,)),
             dma((7,)),
             dma((7,)),
-            dma((ITERS, 2, 4)),
-            dma((ITERS, 2, 4)),
+            dma((ITERS, PARTS, 4)),
+            dma((ITERS, PARTS, 4)),
             dma((ITERS,)),
             dma((ITERS,)),
             dma((ITERS, 16)),

time: 83.6 us -> 82 us (0.981)
  Pallas kernels: 82.9 us -> 81.2 us
    pallas_call x1, Pallas kernels: 79.5 us -> 77.9 us  [per_device(): pl.pallas_call(kernel, out_shape=(jax.ShapeDtypeStruct((blocks, BLK, BLK)...]
where the time goes in v4:
time: 82 us; the launch traced here: 81.9 us
  Pallas kernels  81.2 us (99%)
    pallas_call x1, Pallas kernels, per_device(): pl.pallas_call(kernel, out_shape=(jax.ShapeDtypeStruct((blocks, BLK, BLK)...  77.9 us
    pallas_call x1, Pallas kernels, per_device(): pl.pallas_call(hand_over, out_shape=tuple((jax.ShapeDtypeStruct(x.shape,...  3.36 us

profile of v4, /device:TPU:1, one launch (start us, length us, event | category | flops | bytes accessed | tf_op | source)
XLA Modules:
  0.0 81.9 jit_solution(8950540097804543517)
XLA Ops:
  0.6 77.9 %gromov_step.1 = (f32[64,128,128]{2,1,0:T(8,128)}, f32[32,128]{1,0:T(8,128)}, f32[1,128]{1,0:T(1,128)}) custom-call(s32[2,32]{1,0:T(2,128)} %bitcast.19, s32[3,32]{1,0:T(4,128)} %bitcast.17, s32[3,1,32]{2,1,0:T(1,128)} %bitcast.18, s32[32,128]{1,0:T(8,128)} %bitcast.16, s32[1,128]{1,0:T(1,128)} %weight_hbm.1, f32[64,128,128]{2,1,0:T(8,128)} %bitcast.14, ...), custom_call_target="tpu_custom_call" | custom-call | tf_op jit(solution)/shard_map/gromov_step/pallas_call | solution.py:657
  78.5 3.4 %hand_over.1 = (f32[64,128,128]{2,1,0:T(8,128)}, f32[32,128]{1,0:T(8,128)}, f32[1,128]{1,0:T(1,128)}) custom-call(f32[64,128,128]{2,1,0:T(8,128)} %get-tuple-element.9.cost, f32[32,128]{1,0:T(8,128)} %get-tuple-element.10.source, f32[1,128]{1,0:T(1,128)} %get-tuple-element.11.target), custom_call_target="tpu_custom_call" | custom-call | tf_op jit(solution)/shard_map/hand_over/pallas_call | solution.py:732

commit v5 on v4

--- a/solution.py
+++ b/solution.py
@@ -112,6 +112,7 @@
     gathered,
     far_high,
     far_low,
+    shifted,
     source_float,
     source_rows,
     weight_float,
@@ -476,13 +477,14 @@
             device(0, 0, 0, dx),
         )
 
-    def send_rows(step, part, found):
-        row_lse[step, pl.ds(pl.multiple_of(part * part_rows, part_rows), part_rows), :] = row_result(found)
+    def send_rows(step, part, value):
+        row_lse[step, pl.ds(pl.multiple_of(part * part_rows, part_rows), part_rows), :] = value
         for dx in (2, 1, 3):
             row_copy(step, part, dx).start()
 
     def second_product(part, _):
-        send_rows(0, part, [row_sums(second_row(part * part_rows + inner)) for inner in range(part_rows)])
+        found = [row_sums(second_row(part * part_rows + inner)) for inner in range(part_rows)]
+        send_rows(0, part, row_result(found))
         return 0
 
     lax.fori_loop(0, PARTS, second_product, 0)
@@ -491,33 +493,57 @@
 
     mine = core * 16
     theirs = 16 - mine
+    half = pl.ds(pl.multiple_of(mine, 16), 16)
+    other_half = pl.ds(pl.multiple_of(theirs, 16), 16)
+
     def row_pass(step, part):
-        found = []
-        for row in range(part * part_rows, (part + 1) * part_rows):
-            found.append(
-                row_sums(
-                    [
-                        target_pot[step, slot_at(row, slot)] - scaled[row * SLOTS + slot]
-                        for slot in range(SLOTS)
-                    ]
-                )
-            )
-        send_rows(step, part, found)
-
-    def column_pass(part, best):
-        potentials = source_pot[part * part_rows : (part + 1) * part_rows, :].T
+        totals = []
+        for inner in range(part_rows):
+            row = part * part_rows + inner
+            values = [
+                jnp.exp(shifted[row * SLOTS + slot] + target_pot[step, slot_at(row, slot)]) for slot in range(SLOTS)
+            ]
+            totals.append(jnp.sum(values[0] + values[1], axis=1, keepdims=True))
+        send_rows(step, part, jnp.concatenate(totals, axis=1).T)
+
+    def merge(values):
+        top = functools.reduce(jnp.maximum, values)
+        total = functools.reduce(jnp.add, [jnp.exp(value - top) for value in values])
+        return top + jnp.log(total)
+
+    def add_up(values):
+        return functools.reduce(jnp.add, values)
+
+    def column_part(step, part, found):
+        for dx in (1, 3, 2):
+            row_copy(step, part, dx).wait_recv()
+        rows = pl.ds(pl.multiple_of(part * part_rows, part_rows), part_rows)
+        arrived = [row_lse[step, rows, :]] + [row_land[step, n, rows, :] for n in range(3)]
+        if step == 0:
+            potentials = log_source[rows, :] - merge(arrived)
+        else:
+            potentials = source_pot[rows, :] + (log_source[rows, :] - jnp.log(add_up(arrived)))
+        source_pot[rows, :] = potentials
+        potentials = potentials.T
         for inner in range(part_rows):
             row = part * part_rows + inner
             potential = potentials[:, inner : inner + 1]
             for slot in range(SLOTS):
                 block = row * SLOTS + slot
+                here = position == slot_at(row, slot)
                 scores = potential - scaled[block]
-                top = jnp.max(scores, axis=0, keepdims=True)
-                total = jnp.sum(jnp.exp(scores - top), axis=0, keepdims=True)
-                peaks[block : block + 1, :] = top
-                sums[block : block + 1, :] = total
-                best = jnp.where(position == slot_at(row, slot), jnp.maximum(best, top), best)
-        return best
+                if step < ITERS - 1:
+                    shifted[block] = scores
+                if step == 0:
+                    top = jnp.max(scores, axis=0, keepdims=True)
+                    total = jnp.sum(jnp.exp(scores - top), axis=0, keepdims=True)
+                    peaks[pl.ds(block, 1), :] = top
+                    sums[pl.ds(block, 1), :] = total
+                    found = jnp.where(here, jnp.maximum(found, top), found)
+                else:
+                    values = jnp.exp(scores + target_pot[step, slot_at(row, slot)])
+                    found = found + jnp.where(here, jnp.sum(values, axis=0, keepdims=True), 0.0)
+        return found
 
     def column_result(best):
         best_rows[...] = best.reshape(GB, 1, BLK)
@@ -529,93 +555,61 @@
             total = total + jnp.where(position == slot_at(row, slot), values[block : block + 1, :], 0.0)
         return jnp.where(total > 0.0, best + jnp.log(jnp.maximum(total, 1e-30)), LOW)
 
-    def merge(values):
-        top = functools.reduce(jnp.maximum, values)
-        total = functools.reduce(jnp.add, [jnp.exp(value - top) for value in values])
-        return top + jnp.log(total)
-
-    def iteration(step, _):
-        moved = []
-
-        def move(copy):
-            copy.start()
-            moved.append(copy)
-            return copy
-
-        for part in range(PARTS):
-            pl.when(step > 0)(functools.partial(row_pass, step, part))
-        best = jnp.full((GB, BLK), LOW, f32)
-        for part in range(PARTS):
-            for dx in (1, 3, 2):
-                row_copy(step, part, dx).wait_recv()
-            rows = slice(part * part_rows, (part + 1) * part_rows)
-            arrived = [row_lse[step, rows, :]] + [row_land[step, n, rows, :] for n in range(3)]
-            source_pot[rows, :] = log_source[rows, :] - merge(arrived)
-            best = column_pass(part, best)
-        half_out[step] = column_result(best)
-        move(
-            remote(
-                half_out.at[step, pl.ds(pl.multiple_of(theirs, 16), 16)],
-                half_land.at[step],
-                half_send.at[step],
-                half_recv.at[step],
-                device(0, 0, 1),
-            )
-        ).wait_recv()
-        own = half_out[step, pl.ds(pl.multiple_of(mine, 16), 16), :]
-        merged[step] = merge([own, half_land[step]])
-        row_sent = [row_copy(step, part, dx) for part in range(PARTS) for dx in (1, 2, 3)]
-
-        def exchange(pieces):
-            copies = []
-            for number in FARTHEST_FIRST:
-                src, dst = pieces(number)
-                copies.append(
-                    remote(
-                        src,
-                        dst,
-                        merge_send.at[step, number],
-                        merge_recv.at[step, number],
-                        device(number // 4, number % 4),
-                    )
-                )
-                copies[-1].start()
-            for copy in copies:
-                copy.wait_recv()
-            for copy in copies:
-                copy.wait_send()
-
-        @pl.when(step < ITERS - 1)
-        def _():
-            exchange(lambda number: (merged.at[step], merged_land.at[step, number - 1]))
-            total = merge([merged[step]] + [merged_land[step, n] for n in range(15)])
-            own = log_target[pl.ds(pl.multiple_of(mine, 16), 16), :] - total
-            here = target_pot.at[step + 1, pl.ds(pl.multiple_of(mine, 16), 16)]
+    def exchange(step, pieces):
+        copies = []
+        for number in FARTHEST_FIRST:
+            src, dst = pieces(number)
+            send_at, recv_at = merge_send.at[step, number], merge_recv.at[step, number]
+            copies.append(remote(src, dst, send_at, recv_at, device(number // 4, number % 4)))
+            start(copies[-1])
+        for copy in copies:
+            copy.wait_recv()
+
+    def iteration(step):
+        if step:
+
+            def row_body(part, _):
+                row_pass(step, part)
+                return 0
+
+            lax.fori_loop(0, PARTS, row_body, 0)
+        combine = add_up if step else merge
+        found = jnp.full((GB, BLK), 0.0 if step else LOW, f32)
+        found = lax.fori_loop(0, PARTS, functools.partial(column_part, step), found)
+        half_out[step] = found if step else column_result(found)
+        copy = remote(
+            half_out.at[step, other_half], half_land.at[step], half_send.at[step], half_recv.at[step], device(0, 0, 1)
+        )
+        start(copy)
+        copy.wait_recv()
+        merged[step] = combine([half_out[step, half, :], half_land[step]])
+        if step < ITERS - 1:
+            exchange(step, lambda number: (merged.at[step], merged_land.at[step, number - 1]))
+            total = combine([merged[step]] + [merged_land[step, n] for n in range(15)])
+            if step:
+                own = target_pot[step, half].reshape(16, BLK) + (log_target[half, :] - jnp.log(total))
+            else:
+                own = log_target[half, :] - total
+            here = target_pot.at[step + 1, half]
             here[...] = own.reshape(16, 1, BLK)
             copy = remote(here, here, pot_send.at[step], pot_recv.at[step], device(0, 0, 1))
-            copy.start()
+            start(copy)
             copy.wait_recv()
-            copy.wait_send()
-
-        @pl.when(step == ITERS - 1)
-        def _():
+        else:
             def pieces(number):
                 theirs_at = ((z + number // 4) % 4) * 4 + (y + number % 4) % 4
                 return merged.at[step, pl.ds(theirs_at, 1)], merged_land.at[step, number - 1, pl.ds(0, 1)]
 
-            exchange(pieces)
+            exchange(step, pieces)
             own = z * 4 + y
-            arrived = [merged_land[step, n, 0:1, :] for n in range(15)]
-            total = merge([merged[step, pl.ds(own, 1), :]] + arrived)
-            target_out[...] = (log_target[pl.ds(mine + own, 1), :] - total) * ENTROPY
-
-        for copy in row_sent:
-            copy.wait_send()
-        for copy in moved:
-            copy.wait_send()
-        return 0
-
-    lax.fori_loop(0, ITERS, iteration, 0)
+            total = combine([merged[step, pl.ds(own, 1), :]] + [merged_land[step, n, 0:1, :] for n in range(15)])
+            change = log_target[pl.ds(mine + own, 1), :] - jnp.log(total)
+            target_out[...] = (target_pot[step, mine + own] + change) * ENTROPY
+
+    for step in range(ITERS):
+        iteration(step)
+    for step, part, dx in itertools.product(range(ITERS), range(PARTS), (1, 2, 3)):
+        row_copy(step, part, dx).wait_send()
     source_out[...] = source_pot[...] * ENTROPY
     for copy in started:
         copy.wait_send()
@@ -678,6 +672,7 @@
             pltpu.VMEM((GB * SHARD, BLK), f32),
             pltpu.VMEM((GB * LINKS + 1, BLK, BLK), bf16),
             pltpu.VMEM((GB * LINKS + 1, BLK, BLK), bf16),
+            pltpu.VMEM((blocks, BLK, BLK), f32),
             pltpu.VMEM((ROWS, BLK), f32),
             pltpu.VMEM((ROWS, 1, BLK), f32),
             pltpu.VMEM((1, BLK), f32),

time: 82 us -> 76 us (0.927)
  Pallas kernels: 81.2 us -> 75.3 us
    pallas_call x1, Pallas kernels: 77.9 us -> 71.9 us  [per_device(): pl.pallas_call(kernel, out_shape=(jax.ShapeDtypeStruct((blocks, BLK, BLK)...]
where the time goes in v5:
time: 76 us; the launch traced here: 75.9 us
  Pallas kernels  75.3 us (99%)
    pallas_call x1, Pallas kernels, per_device(): pl.pallas_call(kernel, out_shape=(jax.ShapeDtypeStruct((blocks, BLK, BLK)...  71.9 us
    pallas_call x1, Pallas kernels, per_device(): pl.pallas_call(hand_over, out_shape=tuple((jax.ShapeDtypeStruct(x.shape,...  3.36 us

profile of v5, /device:TPU:1, one launch (start us, length us, event | category | flops | bytes accessed | tf_op | source)
XLA Modules:
  0.0 75.9 jit_solution(4024750503629204440)
XLA Ops:
  0.6 71.9 %gromov_step.1 = (f32[64,128,128]{2,1,0:T(8,128)}, f32[32,128]{1,0:T(8,128)}, f32[1,128]{1,0:T(1,128)}) custom-call(s32[2,32]{1,0:T(2,128)} %bitcast.19, s32[3,32]{1,0:T(4,128)} %bitcast.17, s32[3,1,32]{2,1,0:T(1,128)} %bitcast.18, s32[32,128]{1,0:T(8,128)} %bitcast.16, s32[1,128]{1,0:T(1,128)} %weight_hbm.1, f32[64,128,128]{2,1,0:T(8,128)} %bitcast.14, ...), custom_call_target="tpu_custom_call" | custom-call | tf_op jit(solution)/shard_map/gromov_step/pallas_call | solution.py:651
  72.6 3.4 %hand_over.1 = (f32[64,128,128]{2,1,0:T(8,128)}, f32[32,128]{1,0:T(8,128)}, f32[1,128]{1,0:T(1,128)}) custom-call(f32[64,128,128]{2,1,0:T(8,128)} %get-tuple-element.9.cost, f32[32,128]{1,0:T(8,128)} %get-tuple-element.10.source, f32[1,128]{1,0:T(1,128)} %get-tuple-element.11.target), custom_call_target="tpu_custom_call" | custom-call | tf_op jit(solution)/shard_map/hand_over/pallas_call | solution.py:727

commit v6 on v5

--- a/solution.py
+++ b/solution.py
@@ -72,7 +72,7 @@
 
 
 DELAY = 3
-PARTS = 4
+PARTS = 2
 FARTHEST_FIRST = sorted(range(1, 16), key=lambda n: abs(n // 4 - 2) + abs(n % 4 - 2))
 NUMBER, SENDS, TAKES = gather_plan()
 

time: 76 us -> 75.1 us (0.988)
  Pallas kernels: 75.3 us -> 74.4 us
    pallas_call x1, Pallas kernels: 71.9 us -> 71 us  [per_device(): pl.pallas_call(kernel, out_shape=(jax.ShapeDtypeStruct((blocks, BLK, BLK)...]
where the time goes in v6:
time: 75.1 us; the launch traced here: 75 us
  Pallas kernels  74.4 us (99%)
    pallas_call x1, Pallas kernels, per_device(): pl.pallas_call(kernel, out_shape=(jax.ShapeDtypeStruct((blocks, BLK, BLK)...  71 us
    pallas_call x1, Pallas kernels, per_device(): pl.pallas_call(hand_over, out_shape=tuple((jax.ShapeDtypeStruct(x.shape,...  3.36 us

profile of v6, /device:TPU:1, one launch (start us, length us, event | category | flops | bytes accessed | tf_op | source)
XLA Modules:
  0.0 75.0 jit_solution(4766871382917262598)
XLA Ops:
  0.6 71.0 %gromov_step.1 = (f32[64,128,128]{2,1,0:T(8,128)}, f32[32,128]{1,0:T(8,128)}, f32[1,128]{1,0:T(1,128)}) custom-call(s32[2,32]{1,0:T(2,128)} %bitcast.19, s32[3,32]{1,0:T(4,128)} %bitcast.17, s32[3,1,32]{2,1,0:T(1,128)} %bitcast.18, s32[32,128]{1,0:T(8,128)} %bitcast.16, s32[1,128]{1,0:T(1,128)} %weight_hbm.1, f32[64,128,128]{2,1,0:T(8,128)} %bitcast.14, ...), custom_call_target="tpu_custom_call" | custom-call | tf_op jit(solution)/shard_map/gromov_step/pallas_call | solution.py:651
  71.7 3.4 %hand_over.1 = (f32[64,128,128]{2,1,0:T(8,128)}, f32[32,128]{1,0:T(8,128)}, f32[1,128]{1,0:T(1,128)}) custom-call(f32[64,128,128]{2,1,0:T(8,128)} %get-tuple-element.9.cost, f32[32,128]{1,0:T(8,128)} %get-tuple-element.10.source, f32[1,128]{1,0:T(1,128)} %get-tuple-element.11.target), custom_call_target="tpu_custom_call" | custom-call | tf_op jit(solution)/shard_map/hand_over/pallas_call | solution.py:727
